TPU v7x, 512 devices: a whole 4x8x8 slice. The times are simulated.
512 devices in a mesh: context: 32 (over z, y_lo), tensor: 8 (over x, y_hi), section: 2 (over core).
Axes of the slice: x: 4, y: 8 (y_hi: 2, y_lo: 4; y = y_hi * 4 + y_lo), z: 8, core: 2. Of those that a mesh axis runs over, the one named last changes fastest.
Arguments:
- queries: bfloat16 [2, 8192, 4096], P('section', 'context', 'tensor'), may hold values from -6 to 6
- keys: bfloat16 [2, 8192, 4096], P('section', 'context', 'tensor'), may hold values from -6 to 6
- values: bfloat16 [2, 8192, 4096], P('section', 'context', 'tensor'), may hold values from -6 to 6
- short_filters: float32 [2, 3, 3, 4096], P('section', None, None, 'tensor'), may hold values from -3 to 3
- decay_rates: float32 [2, 16, 4096], P('section', None, 'tensor'), may hold values from 3.0517578e-05 to 0.05
- residues: float32 [2, 16, 4096], P('section', None, 'tensor'), may hold values from -0.078125 to 0.078125
- out_weight: bfloat16 [2, 4096, 4096], P('section', 'tensor', 'context'), may hold values from -0.09375 to 0.09375
- rotation_signs: int32 [2, 4096], P('section', 'tensor'), may hold values from 0 to 1
Outputs:
- passed: bfloat16 [2, 8192, 4096], P('section', 'context', 'tensor')
All inputs are finite; a program needn't handle non-finite values.
Results may differ from a plain program's by a relative error of at most 0.0065.
Values may be sent and summed in bfloat16 or wider, within the bound.
No kernel may reach another device: no remote copies, remote signals or barrier semaphores. Data moves between devices by JAX's collectives and lax.ppermute only.
A program may use at most 64 MiB of HBM per device.

v0:
```python
import math

import jax
import jax.numpy as jnp
from jax import lax
from jax.experimental import pallas as pl
from jax.experimental.pallas import tpu as pltpu
from jax.sharding import PartitionSpec as P

HB = 512
Z = 8
YL = 4
X = 4
YH = 2
TENSOR = X * YH
TAPS = 3
MODES = 16
LANES = 128
SUBS = 8
GROUPS = 4
EDGE = 16
TOKENS_HERE = 256

f32 = jnp.float32
bf16 = jnp.bfloat16


def place():
    context = lax.axis_index("context")
    return context // YL, context % YL


def rounded(value):
    return value.astype(bf16).astype(f32)


def edges_kernel(q_ref, k_ref, v_ref, out_ref, sems):
    edge = out_ref.shape[1]
    copies = []
    for stream, ref in enumerate((q_ref, k_ref, v_ref)):
        copies.append(pltpu.make_async_copy(ref.at[0, ref.shape[1] - edge :, :], out_ref.at[stream], sems.at[stream]))
    for copy in copies:
        copy.start()
    for copy in copies:
        copy.wait()


def states_kernel(
    q_ref, k_ref, v_ref, filter_ref, decay_ref, mixed_ref, query_ref, before_ref, total_ref, first_ref, padded
):
    rows = mixed_ref.shape[0] // GROUPS
    step = rows // SUBS
    padded[0:8, :] = jnp.zeros((8, padded.shape[1]), f32)
    for stream, ref in enumerate((q_ref, k_ref, v_ref)):
        padded[8 : 8 + rows, :] = ref[0].astype(f32)
        taps = [filter_ref[0, stream, i : i + 1, :] for i in range(TAPS)]
        feature = taps[0] * padded[8 : 8 + rows, :]
        feature = feature + taps[1] * padded[7 : 7 + rows, :]
        feature = feature + taps[2] * padded[6 : 6 + rows, :]
        first_ref[stream] = padded[8:16, :]
        for group in range(GROUPS):
            here = slice(group * rows, (group + 1) * rows)
            part = feature[:, group * LANES : (group + 1) * LANES]
            if stream == 0:
                query_ref[here, :] = part
            elif stream == 1:
                mixed_ref[here, :] = part
            else:
                mixed_ref[here, :] = rounded(mixed_ref[here, :] * part)
    for group in range(GROUPS):
        mixed_ref[group * rows : group * rows + 2, :] = jnp.zeros((2, LANES), f32)

    for group in range(GROUPS):
        lanes = slice(group * LANES, (group + 1) * LANES)
        decay = decay_ref[0, :, lanes]
        factor = jnp.exp(-decay)
        factors = [jnp.broadcast_to(factor[m : m + 1, :], (SUBS, LANES)) for m in range(MODES)]

        def advance(i, state):
            x = mixed_ref[pl.ds(group * rows + i, SUBS, stride=step), :]
            return tuple(a * h + x for a, h in zip(factors, state))

        state = lax.fori_loop(0, step, advance, tuple(jnp.zeros((SUBS, LANES), f32) for _ in range(MODES)), unroll=4)
        for m in range(MODES):
            before_ref[group, m] = state[m]
        over = jnp.exp(-decay * step)
        total = jnp.zeros((MODES, LANES), f32)
        for s in range(SUBS):
            end = before_ref[group, :, s, :]
            before_ref[group, :, s, :] = total
            total = over * total + end
        total_ref[:, lanes] = total


def packet_kernel(halo_ref, first_ref, total_ref, filter_ref, decay_ref, packet_ref, fix_ref):
    taps = [[filter_ref[0, stream, i : i + 1, :] for i in range(TAPS)] for stream in range(3)]

    def pair(stream):
        w = taps[stream]
        behind = halo_ref[stream].astype(f32)
        before2, before1 = behind[EDGE - 2 : EDGE - 1, :], behind[EDGE - 1 :, :]
        here0, here1 = first_ref[stream, 0:1, :], first_ref[stream, 1:2, :]
        zero = w[0] * here0 + w[1] * before1 + w[2] * before2
        one = w[0] * here1 + w[1] * here0 + w[2] * before1
        return zero, one

    x0, x1 = [rounded(a * b) for a, b in zip(pair(1), pair(2))]
    decay = decay_ref[0]
    rows = TOKENS_HERE
    total = total_ref[...] + jnp.exp(-decay * (rows - 1)) * x0 + jnp.exp(-decay * (rows - 2)) * x1
    for target in range(Z):
        packet_ref[target] = total
    behind = halo_ref[0].astype(f32)
    w = taps[0]
    fix_ref[0:1, :] = x0
    fix_ref[1:2, :] = x1
    fix_ref[2:3, :] = w[1] * behind[EDGE - 1 :, :]
    fix_ref[3:4, :] = w[2] * behind[EDGE - 2 : EDGE - 1, :]
    fix_ref[4:5, :] = w[2] * behind[EDGE - 1 :, :]
    fix_ref[5:8, :] = jnp.zeros((3, fix_ref.shape[1]), f32)


def carry_kernel(place, packet_ref, decay_ref, *out_refs):
    z, y_lo = place()
    rows = TOKENS_HERE
    decay = decay_ref[0]
    far = jnp.exp(-decay * (YL * rows))
    before = jnp.zeros(decay.shape, f32)
    for plane in range(Z - 1):
        before = jnp.where(plane < z, far * before + packet_ref[plane], before)
    own = packet_ref[z]
    for turn, out_ref in enumerate(out_refs):
        apart = lax.bitwise_xor(y_lo, turn) - y_lo
        reach = (rows * (YL - 1 + apart)).astype(f32)
        total = jnp.exp(-decay * reach) * before
        near = (rows * jnp.maximum(apart - 1, 0)).astype(f32)
        out_ref[...] = total + jnp.where(apart > 0, jnp.exp(-decay * near) * own, 0.0)


def gate_kernel(
    carry0, carry1, carry2, carry3, mixed_ref, query_ref, before_ref, fix_ref, decay_ref, residue_ref, sign_ref, out_ref, gated
):
    rows = mixed_ref.shape[0] // GROUPS
    step = rows // SUBS
    sub = lax.broadcasted_iota(jnp.int32, (SUBS, LANES), 0)
    head = sub == 0
    start = (sub * step).astype(f32)
    for group in range(GROUPS):
        lanes = slice(group * LANES, (group + 1) * LANES)
        decay = decay_ref[0, :, lanes]
        factor = jnp.exp(-decay)
        residue = residue_ref[0, :, lanes]
        carry = (carry0[:, lanes] + carry1[:, lanes]) + (carry2[:, lanes] + carry3[:, lanes])
        fix = [fix_ref[i : i + 1, lanes] for i in range(5)]
        factors, weights, state = [], [], []
        for m in range(MODES):
            row = slice(m, m + 1)
            factors.append(jnp.broadcast_to(factor[row, :], (SUBS, LANES)))
            weights.append(jnp.broadcast_to(residue[row, :], (SUBS, LANES)))
            rate = decay[row, :]
            edge = jnp.exp(-rate * (start - 1.0)) * fix[0] + jnp.exp(-rate * (start - 2.0)) * fix[1]
            entered = before_ref[group, m] + jnp.exp(-rate * start) * carry[row, :]
            state.append(entered + jnp.where(head, 0.0, edge))

        def advance(i, state, extra=None, first=None):
            at = pl.ds(group * rows + i, SUBS, stride=step)
            x = mixed_ref[at, :]
            query = query_ref[at, :]
            if extra is not None:
                x = x + jnp.where(head, extra, 0.0)
                for term in first:
                    query = query + jnp.where(head, term, 0.0)
            state = tuple(a * h + x for a, h in zip(factors, state))
            terms = [w * h for w, h in zip(weights, state)]
            while len(terms) > 1:
                terms = [a + b for a, b in zip(terms[::2], terms[1::2])]
            gated[at, :] = query * rounded(terms[0])
            return state

        state = advance(0, tuple(state), fix[0], fix[2:4])
        state = advance(1, state, fix[1], fix[4:5])
        lax.fori_loop(2, step, advance, state, unroll=2)
    for group in range(GROUPS):
        out_ref[0:rows, group * LANES : (group + 1) * LANES] = gated[group * rows : (group + 1) * rows, :].astype(bf16)
    sign = (2 * sign_ref[...] - 1).astype(f32)
    out_ref[rows:, :] = jnp.broadcast_to(sign, (EDGE, sign.shape[1])).astype(bf16)


def fan_kernel(first_ref, second_ref, out_ref):
    rows = first_ref.shape[0]
    chunk = 128
    for turn, ref in enumerate((first_ref, second_ref)):
        for start in range(0, rows, chunk):
            here = slice(start, start + chunk)
            block = ref[here, :]
            for target in range(out_ref.shape[0]):
                out_ref[target, turn, here, :] = block


def product_kernel(place, own_ref, across_ref, beside_ref, both_ref, w_ref, out_ref):
    _, y_lo = place()
    group = y_lo // 2
    b = lax.rem(y_lo, 2)
    h = lax.rem(lax.axis_index("tensor"), YH)
    rows = out_ref.shape[2]
    near = jnp.concatenate([own_ref[0:rows, :], across_ref[0:rows, :]], axis=1)
    other = jnp.concatenate([beside_ref[0:rows, :], both_ref[0:rows, :]], axis=1)
    for x in range(X):
        tiles = []
        for c in range(2):
            index = lax.rem(group + c, 2)
            tiles.append(jnp.concatenate([w_ref[YH * x + h, index], w_ref[YH * x + 1 - h, index]], axis=0))
        weight = jnp.concatenate(tiles, axis=1)
        out_ref[x, b] = jnp.dot(near, weight, preferred_element_type=f32).astype(bf16)
        out_ref[x, 1 - b] = jnp.dot(other, weight, preferred_element_type=f32).astype(bf16)


def rotate_kernel(in_ref, sign_ref, out_ref):
    rows = out_ref.shape[0]
    chunk = 64
    row = lax.broadcasted_iota(jnp.int32, (LANES, LANES), 0)
    column = lax.broadcasted_iota(jnp.int32, (LANES, LANES), 1)
    parity = row & column
    for shift in (4, 2, 1):
        parity = parity ^ (parity >> shift)
    matrix = (1 - 2 * (parity & 1)).astype(f32).astype(bf16)
    sign = sign_ref[rows : rows + EDGE, :].astype(f32)[0:1, :]
    for start in range(0, rows, chunk):
        here = slice(start, start + chunk)
        sums = []
        for b in range(2):
            total = in_ref[b, here, :].astype(f32)
            for x in range(1, X):
                total = total + in_ref[2 * x + b, here, :].astype(f32)
            sums.append(total)
        parts = []
        for tile in range(HB // LANES):
            c, b = divmod(tile, 2)
            parts.append(sums[b][:, c * LANES : (c + 1) * LANES] * sign[:, tile * LANES : (tile + 1) * LANES])
        for bit in (1, 2):
            parts = [parts[i] + parts[i ^ bit] if not i & bit else parts[i ^ bit] - parts[i] for i in range(len(parts))]
        for tile, part in enumerate(parts):
            high = part.astype(bf16)
            rest = part - high.astype(f32)
            middle = rest.astype(bf16)
            low = (rest - middle.astype(f32)).astype(bf16)
            turned = jnp.dot(low, matrix, preferred_element_type=f32)
            turned = turned + jnp.dot(middle, matrix, preferred_element_type=f32)
            turned = turned + jnp.dot(high, matrix, preferred_element_type=f32)
            out_ref[here, tile * LANES : (tile + 1) * LANES] = (turned * (1.0 / math.sqrt(HB))).astype(bf16)


SMALL = pl.CostEstimate(flops=1, bytes_accessed=1, transcendentals=0)
PARAMS = pltpu.CompilerParams(vmem_limit_bytes=32 * 1024 * 1024)


WIDE = pltpu.CompilerParams(vmem_limit_bytes=60 * 1024 * 1024)


def edges(q, k, v):
    return pl.pallas_call(
        edges_kernel,
        in_specs=[pl.BlockSpec(memory_space=pltpu.HBM)] * 3,
        out_specs=pl.BlockSpec(memory_space=pltpu.HBM),
        out_shape=jax.ShapeDtypeStruct((3, EDGE, q.shape[2]), bf16),
        scratch_shapes=[pltpu.SemaphoreType.DMA((3,))],
        compiler_params=WIDE,
        cost_estimate=SMALL,
        name="edges",
    )(q, k, v)


def states(q, k, v, filters, decay):
    rows, width = q.shape[1:]
    return pl.pallas_call(
        states_kernel,
        out_shape=(
            jax.ShapeDtypeStruct((GROUPS * rows, LANES), f32),
            jax.ShapeDtypeStruct((GROUPS * rows, LANES), f32),
            jax.ShapeDtypeStruct((GROUPS, MODES, SUBS, LANES), f32),
            jax.ShapeDtypeStruct((MODES, width), f32),
            jax.ShapeDtypeStruct((3, 8, width), f32),
        ),
        scratch_shapes=[pltpu.VMEM((rows + 8, width), f32)],
        compiler_params=PARAMS,
        cost_estimate=SMALL,
        name="states",
    )(q, k, v, filters, decay)


def packet(halo, firsts, total, filters, decay):
    width = total.shape[1]
    return pl.pallas_call(
        packet_kernel,
        out_shape=(jax.ShapeDtypeStruct((Z, MODES, width), f32), jax.ShapeDtypeStruct((8, width), f32)),
        compiler_params=PARAMS,
        cost_estimate=SMALL,
        name="packet",
    )(halo, firsts, total, filters, decay)


def fan(first, second):
    return pl.pallas_call(
        fan_kernel,
        out_shape=jax.ShapeDtypeStruct((Z, 2) + first.shape, bf16),
        compiler_params=PARAMS,
        cost_estimate=SMALL,
        name="fan",
    )(first, second)


def carries(packets, decay, place=place):
    return pl.pallas_call(
        lambda *refs: carry_kernel(place, *refs),
        out_shape=(jax.ShapeDtypeStruct(packets.shape[1:], f32),) * YL,
        compiler_params=PARAMS,
        cost_estimate=SMALL,
        name="carries",
    )(packets, decay)


def gate(carry, mixed, query, before, fix, decay, residues, signs):
    return pl.pallas_call(
        gate_kernel,
        out_shape=jax.ShapeDtypeStruct((mixed.shape[0] // GROUPS + EDGE, GROUPS * LANES), bf16),
        scratch_shapes=[pltpu.VMEM(mixed.shape, f32)],
        compiler_params=PARAMS,
        cost_estimate=SMALL,
        name="gate",
    )(*carry, mixed, query, before, fix, decay, residues, signs)


def product(blocks, weight, place=place):
    rows = blocks[0].shape[0] - EDGE
    return pl.pallas_call(
        lambda *refs: product_kernel(place, *refs),
        out_shape=jax.ShapeDtypeStruct((X, 2, rows, 2 * LANES), bf16),
        compiler_params=PARAMS,
        cost_estimate=SMALL,
        name="product",
    )(*blocks, weight)


def rotate(partials, signs):
    rows = partials.shape[1]
    return pl.pallas_call(
        rotate_kernel,
        out_shape=jax.ShapeDtypeStruct((rows, HB), bf16),
        compiler_params=PARAMS,
        cost_estimate=SMALL,
        name="rotate",
    )(partials, signs)


BOTH = ("context", "tensor")


def at(z, yl, x, yh):
    return (z * YL + yl) * TENSOR + x * YH + yh


Z_GROUPS = [[z * YL + y for z in range(Z)] for y in range(YL)]
SQUARES = [
    [at(z, 2 * g + b, x, h) for x in range(X) for b in range(2)] for z in range(Z) for g in range(2) for h in range(YH)
]
EVERY = [(z, y, x, h) for z in range(Z) for y in range(YL) for x in range(X) for h in range(YH)]
ALL = ("context", "tensor", "section")


def exchanged(route):
    return [(2 * a + core, 2 * b + 1 - core) for a, b in route for core in range(2)]


def weight_route(turn):
    return exchanged([(at(z, y, x, h), at(z - z % 2 + h, y ^ (2 * turn), x, z % 2)) for z, y, x, h in EVERY])


def state_route(turn):
    return [(z * YL + y, z * YL + (y ^ turn)) for z in range(Z) for y in range(YL)]


def row_route(b, turn):
    return exchanged([(at(z, y, x, h), at(z, y ^ b, x, h ^ turn)) for z, y, x, h in EVERY])


def shards(queries, keys, values, short_filters, decay_rates, residues, out_weight, rotation_signs):
    halo = lax.ppermute(edges(queries, keys, values), "context", [(i, i + 1) for i in range(Z * YL - 1)])
    mixed, query, before, total, firsts = states(queries, keys, values, short_filters, decay_rates)
    packets, fix = packet(halo, firsts, total, short_filters, decay_rates)
    own, _ = lax.optimization_barrier((out_weight[0], total))
    pieces = [lax.ppermute(own, ALL, weight_route(turn)) for turn in range(2)]
    packets = lax.all_to_all(packets, "context", 0, 0, axis_index_groups=Z_GROUPS)
    weight = fan(*pieces)
    packets, weight = lax.optimization_barrier((packets, weight))
    weight = lax.all_to_all(weight, "context", 0, 0, axis_index_groups=Z_GROUPS)
    carry = carries(packets, decay_rates)
    carry = [carry[0]] + [lax.ppermute(carry[turn], "context", state_route(turn)) for turn in range(1, YL)]
    gated = gate(carry, mixed, query, before, fix, decay_rates, residues, rotation_signs)
    blocks = [lax.ppermute(gated, ALL, row_route(*turn)) for turn in ((0, 0), (0, 1), (1, 0))]
    pair = [(z * YL + y, z * YL + (y ^ 1)) for z in range(Z) for y in range(YL)]
    blocks.append(lax.ppermute(blocks[1], "context", pair))
    partials = product(blocks, weight)
    rows = partials.shape[2]
    partials = lax.all_to_all(partials.reshape(2 * X, rows, -1), BOTH, 0, 0, axis_index_groups=SQUARES)
    return rotate(partials, blocks[0])[None]


def solution(mesh):
    in_specs = (
        P("section", "context", "tensor"),
        P("section", "context", "tensor"),
        P("section", "context", "tensor"),
        P("section", None, None, "tensor"),
        P("section", None, "tensor"),
        P("section", None, "tensor"),
        P("section", "tensor", "context"),
        P("section", "tensor"),
    )
    out_specs = P("section", "context", "tensor")
    return jax.shard_map(shards, mesh=mesh, in_specs=in_specs, out_specs=out_specs, check_vma=False)
```

profile of v0, /device:TPU:16, one launch (start us, length us, event | category | flops | bytes accessed | tf_op | source)
XLA Modules:
  0.0 125.6 jit_solution(8575960568501525561)
XLA Ops:
  0.0 0.0 copy-start.9
  0.0 2.6 %edges.1 = bf16[3,16,512]{2,1,0:T(8,128)(2,1)} custom-call(bf16[1,256,512]{2,1,0:T(8,128)(2,1)} %q_ref.3, bf16[1,256,512]{2,1,0:T(8,128)(2,1)} %k_ref.3, bf16[1,256,512]{2,1,0:T(8,128)(2,1)} %v_ref.3), custom_call_target="tpu_custom_call" | custom-call | flops 1 | bytes 1 | tf_op jit(solution)/shard_map/edges/pallas_call | solution.py:261
  2.6 3.5 %collective-permute-start = (bf16[3,16,512]{2,1,0:T(8,128)(2,1)}, bf16[3,16,512]{2,1,0:T(8,128)(2,1)S(1)}, u32[]{:S(2)}, u32[]{:S(2)}) collective-permute-start(bf16[3,16,512]{2,1,0:T(8,128)(2,1)} %edges.1), channel_id=1, source_target_pairs={{0,16},{16,32},{32,48},{48,64},{64,80},{80,96},{96,112},{112,128},... | collective-permute-start | bytes 147464 | tf_op jit(solution)/shard_map/ppermute | solution.py:387
  6.1 0.7 copy.9.filter_ref
  6.9 0.0 copy-start
  6.9 0.9 copy-done
  7.8 0.0 copy-start.1
  7.8 0.9 copy-done.1
  8.8 0.0 copy-start.2
  8.8 0.9 copy-done.2
  9.7 0.0 copy-start.3
  9.7 0.8 copy-done.3
  10.5 2.1 %states.1 = (f32[1024,128]{1,0:T(8,128)S(1)}, f32[1024,128]{1,0:T(8,128)S(1)}, f32[4,16,8,128]{3,2,1,0:T(8,128)S(1)}, f32[16,512]{1,0:T(8,128)S(1)}, f32[3,8,512]{2,1,0:T(8,128)S(1)}) custom-call(bf16[1,256,512]{2,1,0:T(8,128)(2,1)S(1)} %copy-done, bf16[1,256,512]{2,1,0:T(8,128)(2,1)S(1)} %copy-done.1, bf16[1,256,512]{2,1,0:T(8,128)(2,1)S(1)} %copy-done.2, ...), custom_call_target="tpu_custom_call" | custom-call | flops 1 | bytes 1 | tf_op jit(solution)/shard_map/states/pallas_call | solution.py:275
  12.6 0.0 copy-start.5
  12.6 0.7 copy-done.5
  13.3 0.0 collective-permute-done.halo_ref
  13.3 0.7 packet.1
  14.0 10.3 %all-to-all-start = ((f32[8,16,512]{2,1,0:T(8,128)}), f32[8,16,512]{2,1,0:T(8,128)S(1)}, u32[]{:S(2)}, u32[]{:S(2)}) async-start(f32[8,16,512]{2,1,0:T(8,128)} %get-tuple-element.21), calls=%async_computation | async-start | bytes 524288 | tf_op jit(solution)/shard_map/all_to_all | solution.py:392
  24.3 0.0 copy-done.9
  24.3 1.9 %collective-permute-start.1 = (bf16[512,128]{1,0:T(8,128)(2,1)S(1)}, bf16[512,128]{1,0:T(8,128)(2,1)S(1)}, u32[]{:S(2)}, u32[]{:S(2)}) collective-permute-start(bf16[512,128]{1,0:T(8,128)(2,1)S(1)} %bitcast.4), channel_id=1, source_target_pairs={{0,1},{1,0},{2,65},{3,64},{4,5},{5,4},{6,69},{7,68},{8,9},{9,8},{1... | collective-permute-start | bytes 393224 | tf_op jit(solution)/shard_map/ppermute | solution.py:391
  26.3 2.3 %collective-permute-start.2 = (bf16[512,128]{1,0:T(8,128)(2,1)S(1)}, bf16[512,128]{1,0:T(8,128)(2,1)S(1)}, u32[]{:S(2)}, u32[]{:S(2)}) collective-permute-start(bf16[512,128]{1,0:T(8,128)(2,1)S(1)} %bitcast.5), channel_id=1, source_target_pairs={{0,33},{1,32},{2,97},{3,96},{4,37},{5,36},{6,101},{7,100},{8,41},{... | collective-permute-start | bytes 393224 | tf_op jit(solution)/shard_map/ppermute | solution.py:391
  28.6 0.0 collective-permute-done.1.first_ref
  28.6 7.7 %collective-permute-done.2.second_ref = bf16[512,128]{1,0:T(8,128)(2,1)S(1)} collective-permute-done((bf16[512,128]{1,0:T(8,128)(2,1)S(1)}, bf16[512,128]{1,0:T(8,128)(2,1)S(1)}, u32[]{:S(2)}, u32[]{:S(2)}) %collective-permute-start.2) | collective-permute-done | bytes 131104 | tf_op jit(solution)/shard_map/ppermute | solution.py:391
  36.4 1.6 %fan.1 = bf16[8,2,512,128]{3,2,1,0:T(8,128)(2,1)} custom-call(bf16[512,128]{1,0:T(8,128)(2,1)S(1)} %collective-permute-done.1.first_ref, bf16[512,128]{1,0:T(8,128)(2,1)S(1)} %collective-permute-done.2.second_ref), custom_call_target="tpu_custom_call" | custom-call | flops 1 | bytes 1 | tf_op jit(solution)/shard_map/fan/pallas_call | solution.py:303
  38.0 0.0 copy-start.4
  38.0 0.0 copy-start.7
  38.0 0.0 copy-start.8
  38.0 0.0 all-to-all-done.refs_0_
  38.0 12.2 %all-to-all-start.1 = ((bf16[8,2,512,128]{3,2,1,0:T(8,128)(2,1)}), bf16[8,2,512,128]{3,2,1,0:T(8,128)(2,1)S(1)}, u32[]{:S(2)}, u32[]{:S(2)}) async-start(bf16[8,2,512,128]{3,2,1,0:T(8,128)(2,1)} %fan.1), calls=%async_computation.1 | async-start | bytes 4194304 | tf_op jit(solution)/shard_map/all_to_all | solution.py:395
  50.2 0.0 copy-done.4
  50.2 0.1 carries.1
  50.3 2.3 %collective-permute-start.3 = (f32[16,512]{1,0:T(8,128)S(1)}, f32[16,512]{1,0:T(8,128)S(1)}, u32[]{:S(2)}, u32[]{:S(2)}) collective-permute-start(f32[16,512]{1,0:T(8,128)S(1)} %get-tuple-element.25), channel_id=1, source_target_pairs={{0,16},{16,0},{32,48},{48,32},{64,80},{80,64},{96,112},{112,96},{1... | collective-permute-start | bytes 98312 | tf_op jit(solution)/shard_map/ppermute | solution.py:397
  52.6 5.7 %collective-permute-start.4 = (f32[16,512]{1,0:T(8,128)S(1)}, f32[16,512]{1,0:T(8,128)S(1)}, u32[]{:S(2)}, u32[]{:S(2)}) collective-permute-start(f32[16,512]{1,0:T(8,128)S(1)} %get-tuple-element.26), channel_id=1, source_target_pairs={{0,32},{16,48},{32,0},{48,16},{64,96},{80,112},{96,64},{112,80},{1... | collective-permute-start | bytes 98312 | tf_op jit(solution)/shard_map/ppermute | solution.py:397
  58.4 1.9 %collective-permute-start.5 = (f32[16,512]{1,0:T(8,128)S(1)}, f32[16,512]{1,0:T(8,128)S(1)}, u32[]{:S(2)}, u32[]{:S(2)}) collective-permute-start(f32[16,512]{1,0:T(8,128)S(1)} %get-tuple-element.27), channel_id=1, source_target_pairs={{0,48},{16,32},{32,16},{48,0},{64,112},{80,96},{96,80},{112,64},{1... | collective-permute-start | bytes 98312 | tf_op jit(solution)/shard_map/ppermute | solution.py:397
  60.3 0.0 collective-permute-done.3.carry1
  60.3 0.0 collective-permute-done.4.carry2
  60.3 3.9 %collective-permute-done.5.carry3 = f32[16,512]{1,0:T(8,128)S(1)} collective-permute-done((f32[16,512]{1,0:T(8,128)S(1)}, f32[16,512]{1,0:T(8,128)S(1)}, u32[]{:S(2)}, u32[]{:S(2)}) %collective-permute-start.5) | collective-permute-done | bytes 32800 | tf_op jit(solution)/shard_map/ppermute | solution.py:397
  64.2 0.0 copy-done.7
  64.2 0.0 copy-done.8
  64.2 0.0 copy-start.6
  64.2 0.9 copy-done.6
  65.1 2.5 %gate.1 = bf16[272,512]{1,0:T(8,128)(2,1)S(1)} custom-call(f32[16,512]{1,0:T(8,128)S(1)} %get-tuple-element.24.carry0, f32[16,512]{1,0:T(8,128)S(1)} %collective-permute-done.3.carry1, f32[16,512]{1,0:T(8,128)S(1)} %collective-permute-done.4.carry2, f32[16,512]{1,0:T(8,128)S(1)} %collective-permute-done.5.carry3, ...), custom_call_target="tpu_custom_call" | custom-call | flops 1 | bytes 1 | tf_op jit(solution)/shard_map/gate/pallas_call | solution.py:323
  67.7 4.0 %collective-permute-start.7 = (bf16[272,512]{1,0:T(8,128)(2,1)S(1)}, bf16[272,512]{1,0:T(8,128)(2,1)S(1)}, u32[]{:S(2)}, u32[]{:S(2)}) collective-permute-start(bf16[272,512]{1,0:T(8,128)(2,1)S(1)} %gate.1), channel_id=1, source_target_pairs={{0,3},{1,2},{2,1},{3,0},{4,7},{5,6},{6,5},{7,4},{8,11},{9,10},{10,... | collective-permute-start | bytes 835592 | tf_op jit(solution)/shard_map/ppermute | solution.py:399
  71.6 4.1 %collective-permute-start.6 = (bf16[272,512]{1,0:T(8,128)(2,1)S(1)}, bf16[272,512]{1,0:T(8,128)(2,1)S(1)}, u32[]{:S(2)}, u32[]{:S(2)}) collective-permute-start(bf16[272,512]{1,0:T(8,128)(2,1)S(1)} %gate.1), channel_id=1, source_target_pairs={{0,1},{1,0},{2,3},{3,2},{4,5},{5,4},{6,7},{7,6},{8,9},{9,8},{10,11... | collective-permute-start | bytes 835592 | tf_op jit(solution)/shard_map/ppermute | solution.py:399
  75.7 3.3 %collective-permute-start.8 = (bf16[272,512]{1,0:T(8,128)(2,1)S(1)}, bf16[272,512]{1,0:T(8,128)(2,1)S(1)}, u32[]{:S(2)}, u32[]{:S(2)}) collective-permute-start(bf16[272,512]{1,0:T(8,128)(2,1)S(1)} %gate.1), channel_id=1, source_target_pairs={{0,17},{1,16},{2,19},{3,18},{4,21},{5,20},{6,23},{7,22},{8,25},{9,... | collective-permute-start | bytes 835592 | tf_op jit(solution)/shard_map/ppermute | solution.py:399
  79.1 6.6 %collective-permute-done.7.refs_1_ = bf16[272,512]{1,0:T(8,128)(2,1)S(1)} collective-permute-done((bf16[272,512]{1,0:T(8,128)(2,1)S(1)}, bf16[272,512]{1,0:T(8,128)(2,1)S(1)}, u32[]{:S(2)}, u32[]{:S(2)}) %collective-permute-start.7) | collective-permute-done | bytes 278560 | tf_op jit(solution)/shard_map/ppermute | solution.py:399
  85.7 6.4 %collective-permute-start.9 = (bf16[272,512]{1,0:T(8,128)(2,1)S(1)}, bf16[272,512]{1,0:T(8,128)(2,1)S(1)}, u32[]{:S(2)}, u32[]{:S(2)}) collective-permute-start(bf16[272,512]{1,0:T(8,128)(2,1)S(1)} %collective-permute-done.7.refs_1_), channel_id=1, source_target_pairs={{0,16},{16,0},{32,48},{48,32},{64,80},{80,64},{96,112},{112,96},{1... | collective-permute-start | bytes 835592 | tf_op jit(solution)/shard_map/ppermute | solution.py:401
  92.1 0.0 collective-permute-done.6.refs_0_.sign_ref
  92.1 0.5 collective-permute-done.8.refs_2_
  92.7 6.0 %collective-permute-done.9.refs_3_ = bf16[272,512]{1,0:T(8,128)(2,1)S(1)} collective-permute-done((bf16[272,512]{1,0:T(8,128)(2,1)S(1)}, bf16[272,512]{1,0:T(8,128)(2,1)S(1)}, u32[]{:S(2)}, u32[]{:S(2)}) %collective-permute-start.9) | collective-permute-done | bytes 278560 | tf_op jit(solution)/shard_map/ppermute | solution.py:401
  98.6 4.2 %all-to-all-done.1.refs_4_ = bf16[8,2,512,128]{3,2,1,0:T(8,128)(2,1)S(1)} async-done(((bf16[8,2,512,128]{3,2,1,0:T(8,128)(2,1)}), bf16[8,2,512,128]{3,2,1,0:T(8,128)(2,1)S(1)}, u32[]{:S(2)}, u32[]{:S(2)}) %all-to-all-start.1) | async-done | bytes 2097184 | tf_op jit(solution)/shard_map/all_to_all | solution.py:395
  102.9 1.3 product.1
  104.1 20.1 %all_to_all.15.in_ref = bf16[8,256,256]{2,1,0:T(8,128)(2,1)S(1)} all-to-all(bf16[8,256,256]{2,1,0:T(8,128)(2,1)S(1)} %bitcast.3), channel_id=1, replica_groups={{0,16,4,20,8,24,12,28},{2,18,6,22,10,26,14,30},{32,48,36,52,40,56,44,60..., dimensions={0} | all-to-all | bytes 2097152 | tf_op jit(solution)/shard_map/all_to_all | solution.py:404
  124.3 1.3 %rotate.1 = bf16[256,512]{1,0:T(8,128)(2,1)} custom-call(bf16[8,256,256]{2,1,0:T(8,128)(2,1)S(1)} %all_to_all.15.in_ref, bf16[272,512]{1,0:T(8,128)(2,1)S(1)} %collective-permute-done.6.refs_0_.sign_ref), custom_call_target="tpu_custom_call" | custom-call | flops 1 | bytes 1 | tf_op jit(solution)/shard_map/rotate/pallas_call | solution.py:346
Async XLA Ops:
  0.0 24.3 %copy-start.9 = (bf16[1,512,128]{2,1,0:T(8,128)(2,1)S(1)}, bf16[1,512,128]{2,1,0:T(8,128)(2,1)}, u32[]{:S(2)}) copy-start(bf16[1,512,128]{2,1,0:T(8,128)(2,1)} %param.14) | copy-start | bytes 393220
  2.6 10.7 %collective-permute-start = (bf16[3,16,512]{2,1,0:T(8,128)(2,1)}, bf16[3,16,512]{2,1,0:T(8,128)(2,1)S(1)}, u32[]{:S(2)}, u32[]{:S(2)}) collective-permute-start(bf16[3,16,512]{2,1,0:T(8,128)(2,1)} %edges.1), channel_id=1, source_target_pairs={{0,16},{16,32},{32,48},{48,64},{64,80},{80,96},{96,112},{112,128},... | collective-permute-start | bytes 147464 | tf_op jit(solution)/shard_map/ppermute | solution.py:387
  6.9 0.9 copy-start
  7.8 0.9 copy-start.1
  8.8 0.9 copy-start.2
  9.7 0.8 copy-start.3
  12.6 0.7 copy-start.5
  14.0 23.9 %all-to-all-start = ((f32[8,16,512]{2,1,0:T(8,128)}), f32[8,16,512]{2,1,0:T(8,128)S(1)}, u32[]{:S(2)}, u32[]{:S(2)}) async-start(f32[8,16,512]{2,1,0:T(8,128)} %get-tuple-element.21), calls=%async_computation | async-start | bytes 524288 | tf_op jit(solution)/shard_map/all_to_all | solution.py:392
  24.3 4.3 %collective-permute-start.1 = (bf16[512,128]{1,0:T(8,128)(2,1)S(1)}, bf16[512,128]{1,0:T(8,128)(2,1)S(1)}, u32[]{:S(2)}, u32[]{:S(2)}) collective-permute-start(bf16[512,128]{1,0:T(8,128)(2,1)S(1)} %bitcast.4), channel_id=1, source_target_pairs={{0,1},{1,0},{2,65},{3,64},{4,5},{5,4},{6,69},{7,68},{8,9},{9,8},{1... | collective-permute-start | bytes 393224 | tf_op jit(solution)/shard_map/ppermute | solution.py:391
  26.3 10.1 %collective-permute-start.2 = (bf16[512,128]{1,0:T(8,128)(2,1)S(1)}, bf16[512,128]{1,0:T(8,128)(2,1)S(1)}, u32[]{:S(2)}, u32[]{:S(2)}) collective-permute-start(bf16[512,128]{1,0:T(8,128)(2,1)S(1)} %bitcast.5), channel_id=1, source_target_pairs={{0,33},{1,32},{2,97},{3,96},{4,37},{5,36},{6,101},{7,100},{8,41},{... | collective-permute-start | bytes 393224 | tf_op jit(solution)/shard_map/ppermute | solution.py:391
  38.0 12.2 %copy-start.4 = (f32[1,16,512]{2,1,0:T(8,128)S(1)}, f32[1,16,512]{2,1,0:T(8,128)}, u32[]{:S(2)}) copy-start(f32[1,16,512]{2,1,0:T(8,128)} %decay_ref.5) | copy-start | bytes 98308
  38.0 26.2 %copy-start.7 = (f32[1,16,512]{2,1,0:T(8,128)S(1)}, f32[1,16,512]{2,1,0:T(8,128)}, u32[]{:S(2)}) copy-start(f32[1,16,512]{2,1,0:T(8,128)} %residue_ref.1) | copy-start | bytes 98308
  38.0 26.2 %copy-start.8 = (s32[1,512]{1,0:T(1,128)S(1)}, s32[1,512]{1,0:T(1,128)}, u32[]{:S(2)}) copy-start(s32[1,512]{1,0:T(1,128)} %sign_ref.1) | copy-start | bytes 6148
  38.0 64.9 %all-to-all-start.1 = ((bf16[8,2,512,128]{3,2,1,0:T(8,128)(2,1)}), bf16[8,2,512,128]{3,2,1,0:T(8,128)(2,1)S(1)}, u32[]{:S(2)}, u32[]{:S(2)}) async-start(bf16[8,2,512,128]{3,2,1,0:T(8,128)(2,1)} %fan.1), calls=%async_computation.1 | async-start | bytes 4194304 | tf_op jit(solution)/shard_map/all_to_all | solution.py:395
  50.3 10.0 %collective-permute-start.3 = (f32[16,512]{1,0:T(8,128)S(1)}, f32[16,512]{1,0:T(8,128)S(1)}, u32[]{:S(2)}, u32[]{:S(2)}) collective-permute-start(f32[16,512]{1,0:T(8,128)S(1)} %get-tuple-element.25), channel_id=1, source_target_pairs={{0,16},{16,0},{32,48},{48,32},{64,80},{80,64},{96,112},{112,96},{1... | collective-permute-start | bytes 98312 | tf_op jit(solution)/shard_map/ppermute | solution.py:397
  52.6 7.7 %collective-permute-start.4 = (f32[16,512]{1,0:T(8,128)S(1)}, f32[16,512]{1,0:T(8,128)S(1)}, u32[]{:S(2)}, u32[]{:S(2)}) collective-permute-start(f32[16,512]{1,0:T(8,128)S(1)} %get-tuple-element.26), channel_id=1, source_target_pairs={{0,32},{16,48},{32,0},{48,16},{64,96},{80,112},{96,64},{112,80},{1... | collective-permute-start | bytes 98312 | tf_op jit(solution)/shard_map/ppermute | solution.py:397
  58.4 5.8 %collective-permute-start.5 = (f32[16,512]{1,0:T(8,128)S(1)}, f32[16,512]{1,0:T(8,128)S(1)}, u32[]{:S(2)}, u32[]{:S(2)}) collective-permute-start(f32[16,512]{1,0:T(8,128)S(1)} %get-tuple-element.27), channel_id=1, source_target_pairs={{0,48},{16,32},{32,16},{48,0},{64,112},{80,96},{96,80},{112,64},{1... | collective-permute-start | bytes 98312 | tf_op jit(solution)/shard_map/ppermute | solution.py:397
  64.2 1.0 copy-start.6
  67.7 18.0 %collective-permute-start.7 = (bf16[272,512]{1,0:T(8,128)(2,1)S(1)}, bf16[272,512]{1,0:T(8,128)(2,1)S(1)}, u32[]{:S(2)}, u32[]{:S(2)}) collective-permute-start(bf16[272,512]{1,0:T(8,128)(2,1)S(1)} %gate.1), channel_id=1, source_target_pairs={{0,3},{1,2},{2,1},{3,0},{4,7},{5,6},{6,5},{7,4},{8,11},{9,10},{10,... | collective-permute-start | bytes 835592 | tf_op jit(solution)/shard_map/ppermute | solution.py:399
  71.6 20.5 %collective-permute-start.6 = (bf16[272,512]{1,0:T(8,128)(2,1)S(1)}, bf16[272,512]{1,0:T(8,128)(2,1)S(1)}, u32[]{:S(2)}, u32[]{:S(2)}) collective-permute-start(bf16[272,512]{1,0:T(8,128)(2,1)S(1)} %gate.1), channel_id=1, source_target_pairs={{0,1},{1,0},{2,3},{3,2},{4,5},{5,4},{6,7},{7,6},{8,9},{9,8},{10,11... | collective-permute-start | bytes 835592 | tf_op jit(solution)/shard_map/ppermute | solution.py:399
  75.7 16.9 %collective-permute-start.8 = (bf16[272,512]{1,0:T(8,128)(2,1)S(1)}, bf16[272,512]{1,0:T(8,128)(2,1)S(1)}, u32[]{:S(2)}, u32[]{:S(2)}) collective-permute-start(bf16[272,512]{1,0:T(8,128)(2,1)S(1)} %gate.1), channel_id=1, source_target_pairs={{0,17},{1,16},{2,19},{3,18},{4,21},{5,20},{6,23},{7,22},{8,25},{9,... | collective-permute-start | bytes 835592 | tf_op jit(solution)/shard_map/ppermute | solution.py:399
  85.7 13.0 %collective-permute-start.9 = (bf16[272,512]{1,0:T(8,128)(2,1)S(1)}, bf16[272,512]{1,0:T(8,128)(2,1)S(1)}, u32[]{:S(2)}, u32[]{:S(2)}) collective-permute-start(bf16[272,512]{1,0:T(8,128)(2,1)S(1)} %collective-permute-done.7.refs_1_), channel_id=1, source_target_pairs={{0,16},{16,0},{32,48},{48,32},{64,80},{80,64},{96,112},{112,96},{1... | collective-permute-start | bytes 835592 | tf_op jit(solution)/shard_map/ppermute | solution.py:401
where the time goes:
time: 126 us
  starting transfers between devices  58.1 us (46%)
  waiting for transfers between devices  28.9 us (23%)
  blocking collectives  20.1 us (16%)
  Pallas kernels  12.2 us (10%)
  local copies, waits for them, and re-layouts  6 us (5%)
    all_to_all x1, blocking collectives, shards(): lax.all_to_all(partials.reshape(2 * X, rows, -1), BOTH, 0, 0, axis_index_...  20.1 us
    all_to_all x1, starting transfers between devices, shards(): weight = lax.all_to_all(weight, 'context', 0, 0, axis_index_groups=Z_GROUPS)  12.2 us
    ppermute x3, starting transfers between devices, shards(): lax.ppermute(gated, ALL, row_route(*turn))  11.4 us
    all_to_all x1, starting transfers between devices, shards(): lax.all_to_all(packets, 'context', 0, 0, axis_index_groups=Z_GROUPS)  10.3 us
    ppermute x3, starting transfers between devices, shards(): lax.ppermute(carry[turn], 'context', state_route(turn))  9.99 us
    ppermute x2, waiting for transfers between devices, shards(): pieces = [lax.ppermute(own, ALL, weight_route(turn)) for turn in range(2)]  7.72 us
    ppermute x3, waiting for transfers between devices, shards(): lax.ppermute(gated, ALL, row_route(*turn))  7.13 us
    ppermute x1, starting transfers between devices, shards(): blocks.append(lax.ppermute(blocks[1], 'context', pair))  6.45 us
  transfers between devices with their start and end apart: 12, of which 6 were waited for; matrix products, arithmetic and copies ran while one was open for 1% of the time, Pallas kernels for 5%

commit v1 on v0

--- a/solution.py
+++ b/solution.py
@@ -34,24 +34,15 @@
     return value.astype(bf16).astype(f32)
 
 
-def edges_kernel(q_ref, k_ref, v_ref, out_ref, sems):
-    edge = out_ref.shape[1]
-    copies = []
-    for stream, ref in enumerate((q_ref, k_ref, v_ref)):
-        copies.append(pltpu.make_async_copy(ref.at[0, ref.shape[1] - edge :, :], out_ref.at[stream], sems.at[stream]))
-    for copy in copies:
-        copy.start()
-    for copy in copies:
-        copy.wait()
-
-
 def states_kernel(
-    q_ref, k_ref, v_ref, filter_ref, decay_ref, mixed_ref, query_ref, before_ref, total_ref, first_ref, padded
+    q_ref, k_ref, v_ref, filter_ref, decay_ref, mixed_ref, query_ref, before_ref, total_ref, first_ref, rate_ref, edge_ref, padded
 ):
     rows = mixed_ref.shape[0] // GROUPS
     step = rows // SUBS
+    rate_ref[...] = decay_ref[...]
     padded[0:8, :] = jnp.zeros((8, padded.shape[1]), f32)
     for stream, ref in enumerate((q_ref, k_ref, v_ref)):
+        edge_ref[stream] = ref[0, rows - EDGE :, :]
         padded[8 : 8 + rows, :] = ref[0].astype(f32)
         taps = [filter_ref[0, stream, i : i + 1, :] for i in range(TAPS)]
         feature = taps[0] * padded[8 : 8 + rows, :]
@@ -186,7 +177,9 @@
     out_ref[rows:, :] = jnp.broadcast_to(sign, (EDGE, sign.shape[1])).astype(bf16)
 
 
-def fan_kernel(first_ref, second_ref, out_ref):
+def fan_kernel(first_ref, second_ref, residue_ref, sign_ref, out_ref, residue_out, sign_out):
+    residue_out[...] = residue_ref[...]
+    sign_out[...] = sign_ref[...]
     rows = first_ref.shape[0]
     chunk = 128
     for turn, ref in enumerate((first_ref, second_ref)):
@@ -254,22 +247,6 @@
 PARAMS = pltpu.CompilerParams(vmem_limit_bytes=32 * 1024 * 1024)
 
 
-WIDE = pltpu.CompilerParams(vmem_limit_bytes=60 * 1024 * 1024)
-
-
-def edges(q, k, v):
-    return pl.pallas_call(
-        edges_kernel,
-        in_specs=[pl.BlockSpec(memory_space=pltpu.HBM)] * 3,
-        out_specs=pl.BlockSpec(memory_space=pltpu.HBM),
-        out_shape=jax.ShapeDtypeStruct((3, EDGE, q.shape[2]), bf16),
-        scratch_shapes=[pltpu.SemaphoreType.DMA((3,))],
-        compiler_params=WIDE,
-        cost_estimate=SMALL,
-        name="edges",
-    )(q, k, v)
-
-
 def states(q, k, v, filters, decay):
     rows, width = q.shape[1:]
     return pl.pallas_call(
@@ -280,6 +257,8 @@
             jax.ShapeDtypeStruct((GROUPS, MODES, SUBS, LANES), f32),
             jax.ShapeDtypeStruct((MODES, width), f32),
             jax.ShapeDtypeStruct((3, 8, width), f32),
+            jax.ShapeDtypeStruct(decay.shape, f32),
+            jax.ShapeDtypeStruct((3, EDGE, width), bf16),
         ),
         scratch_shapes=[pltpu.VMEM((rows + 8, width), f32)],
         compiler_params=PARAMS,
@@ -299,14 +278,18 @@
     )(halo, firsts, total, filters, decay)
 
 
-def fan(first, second):
+def fan(first, second, residues, signs):
     return pl.pallas_call(
         fan_kernel,
-        out_shape=jax.ShapeDtypeStruct((Z, 2) + first.shape, bf16),
+        out_shape=(
+            jax.ShapeDtypeStruct((Z, 2) + first.shape, bf16),
+            jax.ShapeDtypeStruct(residues.shape, f32),
+            jax.ShapeDtypeStruct(signs.shape, jnp.int32),
+        ),
         compiler_params=PARAMS,
         cost_estimate=SMALL,
         name="fan",
-    )(first, second)
+    )(first, second, residues, signs)
 
 
 def carries(packets, decay, place=place):
@@ -384,18 +367,18 @@
 
 
 def shards(queries, keys, values, short_filters, decay_rates, residues, out_weight, rotation_signs):
-    halo = lax.ppermute(edges(queries, keys, values), "context", [(i, i + 1) for i in range(Z * YL - 1)])
-    mixed, query, before, total, firsts = states(queries, keys, values, short_filters, decay_rates)
-    packets, fix = packet(halo, firsts, total, short_filters, decay_rates)
-    own, _ = lax.optimization_barrier((out_weight[0], total))
-    pieces = [lax.ppermute(own, ALL, weight_route(turn)) for turn in range(2)]
+    mixed, query, before, total, firsts, rates, edge = states(queries, keys, values, short_filters, decay_rates)
+    halo = lax.ppermute(edge, "context", [(i, i + 1) for i in range(Z * YL - 1)])
+    pieces = [lax.ppermute(out_weight[0], ALL, weight_route(turn)) for turn in range(2)]
+    packets, fix = packet(halo, firsts, total, short_filters, rates)
+    packets, pieces = lax.optimization_barrier((packets, pieces))
     packets = lax.all_to_all(packets, "context", 0, 0, axis_index_groups=Z_GROUPS)
-    weight = fan(*pieces)
+    weight, weights, signs = fan(*pieces, residues, rotation_signs)
     packets, weight = lax.optimization_barrier((packets, weight))
     weight = lax.all_to_all(weight, "context", 0, 0, axis_index_groups=Z_GROUPS)
-    carry = carries(packets, decay_rates)
+    carry = carries(packets, rates)
     carry = [carry[0]] + [lax.ppermute(carry[turn], "context", state_route(turn)) for turn in range(1, YL)]
-    gated = gate(carry, mixed, query, before, fix, decay_rates, residues, rotation_signs)
+    gated = gate(carry, mixed, query, before, fix, rates, weights, signs)
     blocks = [lax.ppermute(gated, ALL, row_route(*turn)) for turn in ((0, 0), (0, 1), (1, 0))]
     pair = [(z * YL + y, z * YL + (y ^ 1)) for z in range(Z) for y in range(YL)]
     blocks.append(lax.ppermute(blocks[1], "context", pair))

time: 126 us -> 121 us (0.960)
  the two profiles are of different devices: /device:TPU:16 before, /device:TPU:8 now
where the time goes in v1:
time: 121 us; the launch traced here: 120 us
  starting transfers between devices  59.6 us (49%)
  waiting for transfers between devices  23.3 us (19%)
  blocking collectives  19.6 us (16%)
  local copies, waits for them, and re-layouts  8.74 us (7%)
  Pallas kernels  8.35 us (7%)
    all_to_all x1, blocking collectives, shards(): lax.all_to_all(partials.reshape(2 * X, rows, -1), BOTH, 0, 0, axis_index_...  19.6 us
    ppermute x3, starting transfers between devices, shards(): lax.ppermute(gated, ALL, row_route(*turn))  13 us
    all_to_all x1, starting transfers between devices, shards(): lax.all_to_all(packets, 'context', 0, 0, axis_index_groups=Z_GROUPS)  11 us
    ppermute x3, starting transfers between devices, shards(): lax.ppermute(carry[turn], 'context', state_route(turn))  10.3 us
    unnamed x19, local copies, waits for them, and re-layouts  8.74 us
    ppermute x1, starting transfers between devices, shards(): blocks.append(lax.ppermute(blocks[1], 'context', pair))  8.45 us
    all_to_all x1, waiting for transfers between devices, shards(): lax.all_to_all(packets, 'context', 0, 0, axis_index_groups=Z_GROUPS)  7.61 us
    ppermute x1, starting transfers between devices, shards(): lax.ppermute(edge, 'context', [(i, i + 1) for i in range(Z * YL - 1)])  6.59 us
  transfers between devices with their start and end apart: 12, of which 8 were waited for; matrix products, arithmetic and copies ran while one was open for 1% of the time, Pallas kernels for 5%

profile of v1, /device:TPU:8, one launch (start us, length us, event | category | flops | bytes accessed | tf_op | source)
XLA Modules:
  0.0 119.8 jit_solution(12556011012590882401)
XLA Ops:
  0.0 1.9 %collective-permute-start.1 = (bf16[512,128]{1,0:T(8,128)(2,1)}, bf16[512,128]{1,0:T(8,128)(2,1)S(1)}, u32[]{:S(2)}, u32[]{:S(2)}) collective-permute-start(bf16[512,128]{1,0:T(8,128)(2,1)} %bitcast.4), channel_id=1, source_target_pairs={{0,1},{1,0},{2,65},{3,64},{4,5},{5,4},{6,69},{7,68},{8,9},{9,8},{1... | collective-permute-start | bytes 393224 | tf_op jit(solution)/shard_map/ppermute | solution.py:372
  1.9 4.6 %collective-permute-start.2 = (bf16[512,128]{1,0:T(8,128)(2,1)}, bf16[512,128]{1,0:T(8,128)(2,1)S(1)}, u32[]{:S(2)}, u32[]{:S(2)}) collective-permute-start(bf16[512,128]{1,0:T(8,128)(2,1)} %bitcast.5), channel_id=1, source_target_pairs={{0,33},{1,32},{2,97},{3,96},{4,37},{5,36},{6,101},{7,100},{8,41},{... | collective-permute-start | bytes 393224 | tf_op jit(solution)/shard_map/ppermute | solution.py:372
  6.5 0.7 copy.9.filter_ref
  7.3 0.0 copy-start.1
  7.3 0.9 copy-done.1
  8.2 0.0 copy-start.2
  8.2 0.9 copy-done.2
  9.2 0.0 copy-start.3
  9.2 0.9 copy-done.3
  10.1 0.0 copy-start.6
  10.1 0.8 copy-done.6
  10.9 2.1 %states.1 = (f32[1024,128]{1,0:T(8,128)S(1)}, f32[1024,128]{1,0:T(8,128)S(1)}, f32[4,16,8,128]{3,2,1,0:T(8,128)S(1)}, f32[16,512]{1,0:T(8,128)S(1)}, f32[3,8,512...) custom-call(bf16[1,256,512]{2,1,0:T(8,128)(2,1)S(1)} %copy-done.1, ...), custom_call_target="tpu_custom_call" | custom-call | flops 1 | bytes 1 | tf_op jit(solution)/shard_map/states/pallas_call | solution.py:252
  13.0 0.0 copy-start.4
  13.0 0.7 copy-done.4
  13.7 6.6 %collective-permute-start = (bf16[3,16,512]{2,1,0:T(8,128)(2,1)S(1)}, bf16[3,16,512]{2,1,0:T(8,128)(2,1)S(1)}, u32[]{:S(2)}, u32[]{:S(2)}) collective-permute-start(bf16[3,16,512]{2,1,0:T(8,128)(2,1)S(1)} %get-tuple-element.26), channel_id=1, source_target_pairs={{0,16},{16,32},{32,48},{48,64},{64,80},{80,96},{96,112},{112,128},... | collective-permute-start | bytes 147464 | tf_op jit(solution)/shard_map/ppermute | solution.py:371
  20.3 2.7 %collective-permute-done.halo_ref = bf16[3,16,512]{2,1,0:T(8,128)(2,1)S(1)} collective-permute-done((bf16[3,16,512]{2,1,0:T(8,128)(2,1)S(1)}, bf16[3,16,512]{2,1,0:T(8,128)(2,1)S(1)}, u32[]{:S(2)}, u32[]{:S(2)}) %collective-permute-start) | collective-permute-done | bytes 49184 | tf_op jit(solution)/shard_map/ppermute | solution.py:371
  23.0 0.7 packet.1
  23.8 0.0 collective-permute-done.1.first_ref
  23.8 0.0 collective-permute-done.2.second_ref
  23.8 11.0 %all-to-all-start = ((f32[8,16,512]{2,1,0:T(8,128)}), f32[8,16,512]{2,1,0:T(8,128)S(1)}, u32[]{:S(2)}, u32[]{:S(2)}) async-start(f32[8,16,512]{2,1,0:T(8,128)} %get-tuple-element.31), calls=%async_computation | async-start | bytes 524288 | tf_op jit(solution)/shard_map/all_to_all | solution.py:375
  34.8 0.0 copy-start.7
  34.8 0.8 copy-done.7
  35.6 0.0 copy-start.8
  35.6 0.7 copy-done.8
  36.2 0.3 fan.1
  36.6 0.0 copy-start
  36.6 1.3 %copy-done = bf16[8,2,512,128]{3,2,1,0:T(8,128)(2,1)} copy-done((bf16[8,2,512,128]{3,2,1,0:T(8,128)(2,1)}, bf16[8,2,512,128]{3,2,1,0:T(8,128)(2,1)S(1)}, u32[]{:S(2)}) %copy-start) | copy-done | bytes 2097176
  37.9 7.6 %all-to-all-done.refs_0_ = f32[8,16,512]{2,1,0:T(8,128)S(1)} async-done(((f32[8,16,512]{2,1,0:T(8,128)}), f32[8,16,512]{2,1,0:T(8,128)S(1)}, u32[]{:S(2)}, u32[]{:S(2)}) %all-to-all-start) | async-done | bytes 262176 | tf_op jit(solution)/shard_map/all_to_all | solution.py:375
  45.5 3.6 %all-to-all-start.1 = ((bf16[8,2,512,128]{3,2,1,0:T(8,128)(2,1)}), bf16[8,2,512,128]{3,2,1,0:T(8,128)(2,1)S(1)}, u32[]{:S(2)}, u32[]{:S(2)}) async-start(bf16[8,2,512,128]{3,2,1,0:T(8,128)(2,1)} %copy-done), calls=%async_computation.1 | async-start | bytes 4194304 | tf_op jit(solution)/shard_map/all_to_all | solution.py:378
  49.1 0.1 carries.1
  49.2 5.1 %collective-permute-start.3 = (f32[16,512]{1,0:T(8,128)S(1)}, f32[16,512]{1,0:T(8,128)S(1)}, u32[]{:S(2)}, u32[]{:S(2)}) collective-permute-start(f32[16,512]{1,0:T(8,128)S(1)} %get-tuple-element.37), channel_id=1, source_target_pairs={{0,16},{16,0},{32,48},{48,32},{64,80},{80,64},{96,112},{112,96},{1... | collective-permute-start | bytes 98312 | tf_op jit(solution)/shard_map/ppermute | solution.py:380
  54.3 1.9 %collective-permute-start.4 = (f32[16,512]{1,0:T(8,128)S(1)}, f32[16,512]{1,0:T(8,128)S(1)}, u32[]{:S(2)}, u32[]{:S(2)}) collective-permute-start(f32[16,512]{1,0:T(8,128)S(1)} %get-tuple-element.38), channel_id=1, source_target_pairs={{0,32},{16,48},{32,0},{48,16},{64,96},{80,112},{96,64},{112,80},{1... | collective-permute-start | bytes 98312 | tf_op jit(solution)/shard_map/ppermute | solution.py:380
  56.2 3.4 %collective-permute-start.5 = (f32[16,512]{1,0:T(8,128)S(1)}, f32[16,512]{1,0:T(8,128)S(1)}, u32[]{:S(2)}, u32[]{:S(2)}) collective-permute-start(f32[16,512]{1,0:T(8,128)S(1)} %get-tuple-element.39), channel_id=1, source_target_pairs={{0,48},{16,32},{32,16},{48,0},{64,112},{80,96},{96,80},{112,64},{1... | collective-permute-start | bytes 98312 | tf_op jit(solution)/shard_map/ppermute | solution.py:380
  59.6 0.0 collective-permute-done.3.carry1
  59.6 1.4 %collective-permute-done.4.carry2 = f32[16,512]{1,0:T(8,128)S(1)} collective-permute-done((f32[16,512]{1,0:T(8,128)S(1)}, f32[16,512]{1,0:T(8,128)S(1)}, u32[]{:S(2)}, u32[]{:S(2)}) %collective-permute-start.4) | collective-permute-done | bytes 32800 | tf_op jit(solution)/shard_map/ppermute | solution.py:380
  61.0 1.0 collective-permute-done.5.carry3
  62.0 0.0 copy-start.5
  62.0 0.9 copy-done.5
  63.0 2.5 %gate.1 = bf16[272,512]{1,0:T(8,128)(2,1)S(1)} custom-call(f32[16,512]{1,0:T(8,128)S(1)} %get-tuple-element.36.carry0, f32[16,512]{1,0:T(8,128)S(1)} %collective-permute-done.3.carry1, f32[16,512]{1,0:T(8,128)S(1)} %collective-permute-done.4.carry2, f32[16,512]{1,0:T(8,128)S(1)} %collective-permute-done.5.carry3, ...), custom_call_target="tpu_custom_call" | custom-call | flops 1 | bytes 1 | tf_op jit(solution)/shard_map/gate/pallas_call | solution.py:306
  65.5 2.5 %collective-permute-start.7 = (bf16[272,512]{1,0:T(8,128)(2,1)S(1)}, bf16[272,512]{1,0:T(8,128)(2,1)S(1)}, u32[]{:S(2)}, u32[]{:S(2)}) collective-permute-start(bf16[272,512]{1,0:T(8,128)(2,1)S(1)} %gate.1), channel_id=1, source_target_pairs={{0,3},{1,2},{2,1},{3,0},{4,7},{5,6},{6,5},{7,4},{8,11},{9,10},{10,... | collective-permute-start | bytes 835592 | tf_op jit(solution)/shard_map/ppermute | solution.py:382
  68.0 6.6 %collective-permute-start.6 = (bf16[272,512]{1,0:T(8,128)(2,1)S(1)}, bf16[272,512]{1,0:T(8,128)(2,1)S(1)}, u32[]{:S(2)}, u32[]{:S(2)}) collective-permute-start(bf16[272,512]{1,0:T(8,128)(2,1)S(1)} %gate.1), channel_id=1, source_target_pairs={{0,1},{1,0},{2,3},{3,2},{4,5},{5,4},{6,7},{7,6},{8,9},{9,8},{10,11... | collective-permute-start | bytes 835592 | tf_op jit(solution)/shard_map/ppermute | solution.py:382
  74.7 3.9 %collective-permute-start.8 = (bf16[272,512]{1,0:T(8,128)(2,1)S(1)}, bf16[272,512]{1,0:T(8,128)(2,1)S(1)}, u32[]{:S(2)}, u32[]{:S(2)}) collective-permute-start(bf16[272,512]{1,0:T(8,128)(2,1)S(1)} %gate.1), channel_id=1, source_target_pairs={{0,17},{1,16},{2,19},{3,18},{4,21},{5,20},{6,23},{7,22},{8,25},{9,... | collective-permute-start | bytes 835592 | tf_op jit(solution)/shard_map/ppermute | solution.py:382
  78.6 2.5 %collective-permute-done.7.refs_1_ = bf16[272,512]{1,0:T(8,128)(2,1)S(1)} collective-permute-done((bf16[272,512]{1,0:T(8,128)(2,1)S(1)}, bf16[272,512]{1,0:T(8,128)(2,1)S(1)}, u32[]{:S(2)}, u32[]{:S(2)}) %collective-permute-start.7) | collective-permute-done | bytes 278560 | tf_op jit(solution)/shard_map/ppermute | solution.py:382
  81.1 8.5 %collective-permute-start.9 = (bf16[272,512]{1,0:T(8,128)(2,1)S(1)}, bf16[272,512]{1,0:T(8,128)(2,1)S(1)}, u32[]{:S(2)}, u32[]{:S(2)}) collective-permute-start(bf16[272,512]{1,0:T(8,128)(2,1)S(1)} %collective-permute-done.7.refs_1_), channel_id=1, source_target_pairs={{0,16},{16,0},{32,48},{48,32},{64,80},{80,64},{96,112},{112,96},{1... | collective-permute-start | bytes 835592 | tf_op jit(solution)/shard_map/ppermute | solution.py:384
  89.5 0.0 collective-permute-done.6.refs_0_.sign_ref
  89.5 0.9 collective-permute-done.8.refs_2_
  90.4 5.8 %collective-permute-done.9.refs_3_ = bf16[272,512]{1,0:T(8,128)(2,1)S(1)} collective-permute-done((bf16[272,512]{1,0:T(8,128)(2,1)S(1)}, bf16[272,512]{1,0:T(8,128)(2,1)S(1)}, u32[]{:S(2)}, u32[]{:S(2)}) %collective-permute-start.9) | collective-permute-done | bytes 278560 | tf_op jit(solution)/shard_map/ppermute | solution.py:384
  96.3 1.3 %all-to-all-done.1.refs_4_ = bf16[8,2,512,128]{3,2,1,0:T(8,128)(2,1)S(1)} async-done(((bf16[8,2,512,128]{3,2,1,0:T(8,128)(2,1)}), bf16[8,2,512,128]{3,2,1,0:T(8,128)(2,1)S(1)}, u32[]{:S(2)}, u32[]{:S(2)}) %all-to-all-start.1) | async-done | bytes 2097184 | tf_op jit(solution)/shard_map/all_to_all | solution.py:378
  97.6 1.3 %product.1 = bf16[4,2,256,256]{3,2,1,0:T(8,128)(2,1)S(1)} custom-call(bf16[272,512]{1,0:T(8,128)(2,1)S(1)} %collective-permute-done.6.refs_0_.sign_ref, bf16[272,512]{1,0:T(8,128)(2,1)S(1)} %collective-permute-done.7.refs_1_, bf16[272,512]{1,0:T(8,128)(2,1)S(1)} %collective-permute-done.8.refs_2_, bf16[272,512]{1,0:T(8,128)(2,1)S(1)} %collective-permute-done.9.refs_3_, ...), custom_call_target="tpu_custom_call" | custom-call | flops 1 | bytes 1 | tf_op jit(solution)/shard_map/product/pallas_call | solution.py:318
  98.9 19.6 %all_to_all.15.in_ref = bf16[8,256,256]{2,1,0:T(8,128)(2,1)S(1)} all-to-all(bf16[8,256,256]{2,1,0:T(8,128)(2,1)S(1)} %bitcast.3), channel_id=1, replica_groups={{0,16,4,20,8,24,12,28},{2,18,6,22,10,26,14,30},{32,48,36,52,40,56,44,60..., dimensions={0} | all-to-all | bytes 2097152 | tf_op jit(solution)/shard_map/all_to_all | solution.py:387
  118.5 1.3 %rotate.1 = bf16[256,512]{1,0:T(8,128)(2,1)} custom-call(bf16[8,256,256]{2,1,0:T(8,128)(2,1)S(1)} %all_to_all.15.in_ref, bf16[272,512]{1,0:T(8,128)(2,1)S(1)} %collective-permute-done.6.refs_0_.sign_ref), custom_call_target="tpu_custom_call" | custom-call | flops 1 | bytes 1 | tf_op jit(solution)/shard_map/rotate/pallas_call | solution.py:329
Async XLA Ops:
  0.0 23.8 %collective-permute-start.1 = (bf16[512,128]{1,0:T(8,128)(2,1)}, bf16[512,128]{1,0:T(8,128)(2,1)S(1)}, u32[]{:S(2)}, u32[]{:S(2)}) collective-permute-start(bf16[512,128]{1,0:T(8,128)(2,1)} %bitcast.4), channel_id=1, source_target_pairs={{0,1},{1,0},{2,65},{3,64},{4,5},{5,4},{6,69},{7,68},{8,9},{9,8},{1... | collective-permute-start | bytes 393224 | tf_op jit(solution)/shard_map/ppermute | solution.py:372
  1.9 21.9 %collective-permute-start.2 = (bf16[512,128]{1,0:T(8,128)(2,1)}, bf16[512,128]{1,0:T(8,128)(2,1)S(1)}, u32[]{:S(2)}, u32[]{:S(2)}) collective-permute-start(bf16[512,128]{1,0:T(8,128)(2,1)} %bitcast.5), channel_id=1, source_target_pairs={{0,33},{1,32},{2,97},{3,96},{4,37},{5,36},{6,101},{7,100},{8,41},{... | collective-permute-start | bytes 393224 | tf_op jit(solution)/shard_map/ppermute | solution.py:372
  7.3 0.9 copy-start.1
  8.2 0.9 copy-start.2
  9.2 0.9 copy-start.3
  10.1 0.8 copy-start.6
  13.0 0.7 copy-start.4
  13.7 9.3 %collective-permute-start = (bf16[3,16,512]{2,1,0:T(8,128)(2,1)S(1)}, bf16[3,16,512]{2,1,0:T(8,128)(2,1)S(1)}, u32[]{:S(2)}, u32[]{:S(2)}) collective-permute-start(bf16[3,16,512]{2,1,0:T(8,128)(2,1)S(1)} %get-tuple-element.26), channel_id=1, source_target_pairs={{0,16},{16,32},{32,48},{48,64},{64,80},{80,96},{96,112},{112,128},... | collective-permute-start | bytes 147464 | tf_op jit(solution)/shard_map/ppermute | solution.py:371
  23.8 21.8 %all-to-all-start = ((f32[8,16,512]{2,1,0:T(8,128)}), f32[8,16,512]{2,1,0:T(8,128)S(1)}, u32[]{:S(2)}, u32[]{:S(2)}) async-start(f32[8,16,512]{2,1,0:T(8,128)} %get-tuple-element.31), calls=%async_computation | async-start | bytes 524288 | tf_op jit(solution)/shard_map/all_to_all | solution.py:375
  34.8 0.8 copy-start.7
  35.6 0.7 copy-start.8
  36.6 1.3 %copy-start = (bf16[8,2,512,128]{3,2,1,0:T(8,128)(2,1)}, bf16[8,2,512,128]{3,2,1,0:T(8,128)(2,1)S(1)}, u32[]{:S(2)}) copy-start(bf16[8,2,512,128]{3,2,1,0:T(8,128)(2,1)S(1)} %get-tuple-element.46) | copy-start | bytes 6291460
  45.5 52.1 %all-to-all-start.1 = ((bf16[8,2,512,128]{3,2,1,0:T(8,128)(2,1)}), bf16[8,2,512,128]{3,2,1,0:T(8,128)(2,1)S(1)}, u32[]{:S(2)}, u32[]{:S(2)}) async-start(bf16[8,2,512,128]{3,2,1,0:T(8,128)(2,1)} %copy-done), calls=%async_computation.1 | async-start | bytes 4194304 | tf_op jit(solution)/shard_map/all_to_all | solution.py:378
  49.2 10.4 %collective-permute-start.3 = (f32[16,512]{1,0:T(8,128)S(1)}, f32[16,512]{1,0:T(8,128)S(1)}, u32[]{:S(2)}, u32[]{:S(2)}) collective-permute-start(f32[16,512]{1,0:T(8,128)S(1)} %get-tuple-element.37), channel_id=1, source_target_pairs={{0,16},{16,0},{32,48},{48,32},{64,80},{80,64},{96,112},{112,96},{1... | collective-permute-start | bytes 98312 | tf_op jit(solution)/shard_map/ppermute | solution.py:380
  54.3 6.7 %collective-permute-start.4 = (f32[16,512]{1,0:T(8,128)S(1)}, f32[16,512]{1,0:T(8,128)S(1)}, u32[]{:S(2)}, u32[]{:S(2)}) collective-permute-start(f32[16,512]{1,0:T(8,128)S(1)} %get-tuple-element.38), channel_id=1, source_target_pairs={{0,32},{16,48},{32,0},{48,16},{64,96},{80,112},{96,64},{112,80},{1... | collective-permute-start | bytes 98312 | tf_op jit(solution)/shard_map/ppermute | solution.py:380
  56.2 5.8 %collective-permute-start.5 = (f32[16,512]{1,0:T(8,128)S(1)}, f32[16,512]{1,0:T(8,128)S(1)}, u32[]{:S(2)}, u32[]{:S(2)}) collective-permute-start(f32[16,512]{1,0:T(8,128)S(1)} %get-tuple-element.39), channel_id=1, source_target_pairs={{0,48},{16,32},{32,16},{48,0},{64,112},{80,96},{96,80},{112,64},{1... | collective-permute-start | bytes 98312 | tf_op jit(solution)/shard_map/ppermute | solution.py:380
  62.0 1.0 copy-start.5
  65.5 15.5 %collective-permute-start.7 = (bf16[272,512]{1,0:T(8,128)(2,1)S(1)}, bf16[272,512]{1,0:T(8,128)(2,1)S(1)}, u32[]{:S(2)}, u32[]{:S(2)}) collective-permute-start(bf16[272,512]{1,0:T(8,128)(2,1)S(1)} %gate.1), channel_id=1, source_target_pairs={{0,3},{1,2},{2,1},{3,0},{4,7},{5,6},{6,5},{7,4},{8,11},{9,10},{10,... | collective-permute-start | bytes 835592 | tf_op jit(solution)/shard_map/ppermute | solution.py:382
  68.0 21.5 %collective-permute-start.6 = (bf16[272,512]{1,0:T(8,128)(2,1)S(1)}, bf16[272,512]{1,0:T(8,128)(2,1)S(1)}, u32[]{:S(2)}, u32[]{:S(2)}) collective-permute-start(bf16[272,512]{1,0:T(8,128)(2,1)S(1)} %gate.1), channel_id=1, source_target_pairs={{0,1},{1,0},{2,3},{3,2},{4,5},{5,4},{6,7},{7,6},{8,9},{9,8},{10,11... | collective-permute-start | bytes 835592 | tf_op jit(solution)/shard_map/ppermute | solution.py:382
  74.7 15.8 %collective-permute-start.8 = (bf16[272,512]{1,0:T(8,128)(2,1)S(1)}, bf16[272,512]{1,0:T(8,128)(2,1)S(1)}, u32[]{:S(2)}, u32[]{:S(2)}) collective-permute-start(bf16[272,512]{1,0:T(8,128)(2,1)S(1)} %gate.1), channel_id=1, source_target_pairs={{0,17},{1,16},{2,19},{3,18},{4,21},{5,20},{6,23},{7,22},{8,25},{9,... | collective-permute-start | bytes 835592 | tf_op jit(solution)/shard_map/ppermute | solution.py:382
  81.1 15.2 %collective-permute-start.9 = (bf16[272,512]{1,0:T(8,128)(2,1)S(1)}, bf16[272,512]{1,0:T(8,128)(2,1)S(1)}, u32[]{:S(2)}, u32[]{:S(2)}) collective-permute-start(bf16[272,512]{1,0:T(8,128)(2,1)S(1)} %collective-permute-done.7.refs_1_), channel_id=1, source_target_pairs={{0,16},{16,0},{32,48},{48,32},{64,80},{80,64},{96,112},{112,96},{1... | collective-permute-start | bytes 835592 | tf_op jit(solution)/shard_map/ppermute | solution.py:384

commit v2 on v1

--- a/solution.py
+++ b/solution.py
@@ -177,9 +177,7 @@
     out_ref[rows:, :] = jnp.broadcast_to(sign, (EDGE, sign.shape[1])).astype(bf16)
 
 
-def fan_kernel(first_ref, second_ref, residue_ref, sign_ref, out_ref, residue_out, sign_out):
-    residue_out[...] = residue_ref[...]
-    sign_out[...] = sign_ref[...]
+def fan_kernel(first_ref, second_ref, out_ref):
     rows = first_ref.shape[0]
     chunk = 128
     for turn, ref in enumerate((first_ref, second_ref)):
@@ -249,6 +247,7 @@
 
 def states(q, k, v, filters, decay):
     rows, width = q.shape[1:]
+    q, k, v, decay = [pltpu.with_memory_space_constraint(a, pltpu.HBM) for a in (q, k, v, decay)]
     return pl.pallas_call(
         states_kernel,
         out_shape=(
@@ -278,18 +277,14 @@
     )(halo, firsts, total, filters, decay)
 
 
-def fan(first, second, residues, signs):
+def fan(first, second):
     return pl.pallas_call(
         fan_kernel,
-        out_shape=(
-            jax.ShapeDtypeStruct((Z, 2) + first.shape, bf16),
-            jax.ShapeDtypeStruct(residues.shape, f32),
-            jax.ShapeDtypeStruct(signs.shape, jnp.int32),
-        ),
+        out_shape=jax.ShapeDtypeStruct((Z, 2) + first.shape, bf16),
         compiler_params=PARAMS,
         cost_estimate=SMALL,
         name="fan",
-    )(first, second, residues, signs)
+    )(first, second)
 
 
 def carries(packets, decay, place=place):
@@ -303,6 +298,8 @@
 
 
 def gate(carry, mixed, query, before, fix, decay, residues, signs):
+    residues, signs = [pltpu.with_memory_space_constraint(a, pltpu.HBM) for a in (residues, signs)]
+    before = pltpu.with_memory_space_constraint(before, pltpu.VMEM)
     return pl.pallas_call(
         gate_kernel,
         out_shape=jax.ShapeDtypeStruct((mixed.shape[0] // GROUPS + EDGE, GROUPS * LANES), bf16),
@@ -373,12 +370,12 @@
     packets, fix = packet(halo, firsts, total, short_filters, rates)
     packets, pieces = lax.optimization_barrier((packets, pieces))
     packets = lax.all_to_all(packets, "context", 0, 0, axis_index_groups=Z_GROUPS)
-    weight, weights, signs = fan(*pieces, residues, rotation_signs)
+    weight = fan(*pieces)
     packets, weight = lax.optimization_barrier((packets, weight))
     weight = lax.all_to_all(weight, "context", 0, 0, axis_index_groups=Z_GROUPS)
     carry = carries(packets, rates)
     carry = [carry[0]] + [lax.ppermute(carry[turn], "context", state_route(turn)) for turn in range(1, YL)]
-    gated = gate(carry, mixed, query, before, fix, rates, weights, signs)
+    gated = gate(carry, mixed, query, before, fix, rates, residues, rotation_signs)
     blocks = [lax.ppermute(gated, ALL, row_route(*turn)) for turn in ((0, 0), (0, 1), (1, 0))]
     pair = [(z * YL + y, z * YL + (y ^ 1)) for z in range(Z) for y in range(YL)]
     blocks.append(lax.ppermute(blocks[1], "context", pair))

time: 121 us -> 120 us (level)
  the two profiles are of different devices: /device:TPU:8 before, /device:TPU:40 now
where the time goes in v2:
time: 120 us; the launch traced here: 119 us
  starting transfers between devices  55.9 us (47%)
  waiting for transfers between devices  29.2 us (24%)
  blocking collectives  20.2 us (17%)
  Pallas kernels  11.5 us (10%)
  local copies, waits for them, and re-layouts  2.39 us (2%)
    all_to_all x1, blocking collectives, shards(): lax.all_to_all(partials.reshape(2 * X, rows, -1), BOTH, 0, 0, axis_index_...  20.2 us
    ppermute x3, starting transfers between devices, shards(): lax.ppermute(carry[turn], 'context', state_route(turn))  10.9 us
    all_to_all x1, waiting for transfers between devices, shards(): lax.all_to_all(packets, 'context', 0, 0, axis_index_groups=Z_GROUPS)  10.5 us
    all_to_all x1, starting transfers between devices, shards(): lax.all_to_all(packets, 'context', 0, 0, axis_index_groups=Z_GROUPS)  10.3 us
    ppermute x1, starting transfers between devices, shards(): blocks.append(lax.ppermute(blocks[1], 'context', pair))  9.77 us
    ppermute x2, starting transfers between devices, shards(): lax.ppermute(out_weight[0], ALL, weight_route(turn))  8.79 us
    ppermute x3, starting transfers between devices, shards(): lax.ppermute(gated, ALL, row_route(*turn))  8.55 us
    ppermute x1, waiting for transfers between devices, shards(): blocks.append(lax.ppermute(blocks[1], 'context', pair))  5.97 us
  transfers between devices with their start and end apart: 12, of which 9 were waited for; matrix products, arithmetic and copies ran while one was open for 1% of the time, Pallas kernels for 7%

profile of v2, /device:TPU:40, one launch (start us, length us, event | category | flops | bytes accessed | tf_op | source)
XLA Modules:
  0.0 119.4 jit_solution(9164385074656494608)
XLA Ops:
  0.0 4.2 %collective-permute-start.1 = (bf16[512,128]{1,0:T(8,128)(2,1)}, bf16[512,128]{1,0:T(8,128)(2,1)S(1)}, u32[]{:S(2)}, u32[]{:S(2)}) collective-permute-start(bf16[512,128]{1,0:T(8,128)(2,1)} %bitcast.4), channel_id=1, source_target_pairs={{0,1},{1,0},{2,65},{3,64},{4,5},{5,4},{6,69},{7,68},{8,9},{9,8},{1... | collective-permute-start | bytes 393224 | tf_op jit(solution)/shard_map/ppermute | solution.py:369
  4.2 4.6 %collective-permute-start.2 = (bf16[512,128]{1,0:T(8,128)(2,1)}, bf16[512,128]{1,0:T(8,128)(2,1)S(1)}, u32[]{:S(2)}, u32[]{:S(2)}) collective-permute-start(bf16[512,128]{1,0:T(8,128)(2,1)} %bitcast.5), channel_id=1, source_target_pairs={{0,33},{1,32},{2,97},{3,96},{4,37},{5,36},{6,101},{7,100},{8,41},{... | collective-permute-start | bytes 393224 | tf_op jit(solution)/shard_map/ppermute | solution.py:369
  8.8 0.7 copy.9.filter_ref
  9.5 3.2 %states.1 = (f32[1024,128]{1,0:T(8,128)S(1)}, f32[1024,128]{1,0:T(8,128)S(1)}, f32[4,16,8,128]{3,2,1,0:T(8,128)S(1)}, f32[16,512]{1,0:T(8,128)S(1)}, f32[3,8,512...) custom-call(bf16[1,256,512]{2,1,0:T(8,128)(2,1)} %q_ref.1, bf16[1,256,512]{2,1,0:T(8,128)(2,1)} %k_ref.1, ...), custom_call_target="tpu_custom_call" | custom-call | flops 1 | bytes 1 | tf_op jit(solution)/shard_map/states/pallas_call | solution.py:251
  12.8 0.0 copy-start
  12.8 0.7 copy-done
  13.5 3.9 %collective-permute-start = (bf16[3,16,512]{2,1,0:T(8,128)(2,1)S(1)}, bf16[3,16,512]{2,1,0:T(8,128)(2,1)S(1)}, u32[]{:S(2)}, u32[]{:S(2)}) collective-permute-start(bf16[3,16,512]{2,1,0:T(8,128)(2,1)S(1)} %get-tuple-element.23), channel_id=1, source_target_pairs={{0,16},{16,32},{32,48},{48,64},{64,80},{80,96},{96,112},{112,128},... | collective-permute-start | bytes 147464 | tf_op jit(solution)/shard_map/ppermute | solution.py:368
  17.4 2.0 %collective-permute-done.halo_ref = bf16[3,16,512]{2,1,0:T(8,128)(2,1)S(1)} collective-permute-done((bf16[3,16,512]{2,1,0:T(8,128)(2,1)S(1)}, bf16[3,16,512]{2,1,0:T(8,128)(2,1)S(1)}, u32[]{:S(2)}, u32[]{:S(2)}) %collective-permute-start) | collective-permute-done | bytes 49184 | tf_op jit(solution)/shard_map/ppermute | solution.py:368
  19.4 0.7 packet.1
  20.2 0.0 collective-permute-done.1.first_ref
  20.2 0.1 collective-permute-done.2.second_ref
  20.3 10.3 %all-to-all-start = ((f32[8,16,512]{2,1,0:T(8,128)}), f32[8,16,512]{2,1,0:T(8,128)S(1)}, u32[]{:S(2)}, u32[]{:S(2)}) async-start(f32[8,16,512]{2,1,0:T(8,128)} %get-tuple-element.28), calls=%async_computation | async-start | bytes 524288 | tf_op jit(solution)/shard_map/all_to_all | solution.py:372
  30.6 1.6 %fan.1 = bf16[8,2,512,128]{3,2,1,0:T(8,128)(2,1)} custom-call(bf16[512,128]{1,0:T(8,128)(2,1)S(1)} %collective-permute-done.1.first_ref, bf16[512,128]{1,0:T(8,128)(2,1)S(1)} %collective-permute-done.2.second_ref), custom_call_target="tpu_custom_call" | custom-call | flops 1 | bytes 1 | tf_op jit(solution)/shard_map/fan/pallas_call | solution.py:281
  32.2 10.5 %all-to-all-done.refs_0_ = f32[8,16,512]{2,1,0:T(8,128)S(1)} async-done(((f32[8,16,512]{2,1,0:T(8,128)}), f32[8,16,512]{2,1,0:T(8,128)S(1)}, u32[]{:S(2)}, u32[]{:S(2)}) %all-to-all-start) | async-done | bytes 262176 | tf_op jit(solution)/shard_map/all_to_all | solution.py:372
  42.7 3.6 %all-to-all-start.1 = ((bf16[8,2,512,128]{3,2,1,0:T(8,128)(2,1)}), bf16[8,2,512,128]{3,2,1,0:T(8,128)(2,1)S(1)}, u32[]{:S(2)}, u32[]{:S(2)}) async-start(bf16[8,2,512,128]{3,2,1,0:T(8,128)(2,1)} %fan.1), calls=%async_computation.1 | async-start | bytes 4194304 | tf_op jit(solution)/shard_map/all_to_all | solution.py:375
  46.3 0.1 carries.1
  46.4 5.7 %collective-permute-start.3 = (f32[16,512]{1,0:T(8,128)S(1)}, f32[16,512]{1,0:T(8,128)S(1)}, u32[]{:S(2)}, u32[]{:S(2)}) collective-permute-start(f32[16,512]{1,0:T(8,128)S(1)} %get-tuple-element.33), channel_id=1, source_target_pairs={{0,16},{16,0},{32,48},{48,32},{64,80},{80,64},{96,112},{112,96},{1... | collective-permute-start | bytes 98312 | tf_op jit(solution)/shard_map/ppermute | solution.py:377
  52.1 1.9 %collective-permute-start.4 = (f32[16,512]{1,0:T(8,128)S(1)}, f32[16,512]{1,0:T(8,128)S(1)}, u32[]{:S(2)}, u32[]{:S(2)}) collective-permute-start(f32[16,512]{1,0:T(8,128)S(1)} %get-tuple-element.34), channel_id=1, source_target_pairs={{0,32},{16,48},{32,0},{48,16},{64,96},{80,112},{96,64},{112,80},{1... | collective-permute-start | bytes 98312 | tf_op jit(solution)/shard_map/ppermute | solution.py:377
  54.0 3.4 %collective-permute-start.5 = (f32[16,512]{1,0:T(8,128)S(1)}, f32[16,512]{1,0:T(8,128)S(1)}, u32[]{:S(2)}, u32[]{:S(2)}) collective-permute-start(f32[16,512]{1,0:T(8,128)S(1)} %get-tuple-element.35), channel_id=1, source_target_pairs={{0,48},{16,32},{32,16},{48,0},{64,112},{80,96},{96,80},{112,64},{1... | collective-permute-start | bytes 98312 | tf_op jit(solution)/shard_map/ppermute | solution.py:377
  57.4 0.0 collective-permute-done.3.carry1
  57.4 1.4 %collective-permute-done.4.carry2 = f32[16,512]{1,0:T(8,128)S(1)} collective-permute-done((f32[16,512]{1,0:T(8,128)S(1)}, f32[16,512]{1,0:T(8,128)S(1)}, u32[]{:S(2)}, u32[]{:S(2)}) %collective-permute-start.4) | collective-permute-done | bytes 32800 | tf_op jit(solution)/shard_map/ppermute | solution.py:377
  58.8 1.0 collective-permute-done.5.carry3
  59.8 0.0 copy-start.1
  59.8 0.9 copy-done.1
  60.8 3.3 %gate.1 = bf16[272,512]{1,0:T(8,128)(2,1)S(1)} custom-call(f32[16,512]{1,0:T(8,128)S(1)} %get-tuple-element.32.carry0, f32[16,512]{1,0:T(8,128)S(1)} %collective-permute-done.3.carry1, f32[16,512]{1,0:T(8,128)S(1)} %collective-permute-done.4.carry2, f32[16,512]{1,0:T(8,128)S(1)} %collective-permute-done.5.carry3, ...), custom_call_target="tpu_custom_call" | custom-call | flops 1 | bytes 1 | tf_op jit(solution)/shard_map/gate/pallas_call | solution.py:303
  64.1 1.9 %collective-permute-start.7 = (bf16[272,512]{1,0:T(8,128)(2,1)S(1)}, bf16[272,512]{1,0:T(8,128)(2,1)S(1)}, u32[]{:S(2)}, u32[]{:S(2)}) collective-permute-start(bf16[272,512]{1,0:T(8,128)(2,1)S(1)} %gate.1), channel_id=1, source_target_pairs={{0,3},{1,2},{2,1},{3,0},{4,7},{5,6},{6,5},{7,4},{8,11},{9,10},{10,... | collective-permute-start | bytes 835592 | tf_op jit(solution)/shard_map/ppermute | solution.py:379
  66.0 2.7 %collective-permute-start.6 = (bf16[272,512]{1,0:T(8,128)(2,1)S(1)}, bf16[272,512]{1,0:T(8,128)(2,1)S(1)}, u32[]{:S(2)}, u32[]{:S(2)}) collective-permute-start(bf16[272,512]{1,0:T(8,128)(2,1)S(1)} %gate.1), channel_id=1, source_target_pairs={{0,1},{1,0},{2,3},{3,2},{4,5},{5,4},{6,7},{7,6},{8,9},{9,8},{10,11... | collective-permute-start | bytes 835592 | tf_op jit(solution)/shard_map/ppermute | solution.py:379
  68.7 3.9 %collective-permute-start.8 = (bf16[272,512]{1,0:T(8,128)(2,1)S(1)}, bf16[272,512]{1,0:T(8,128)(2,1)S(1)}, u32[]{:S(2)}, u32[]{:S(2)}) collective-permute-start(bf16[272,512]{1,0:T(8,128)(2,1)S(1)} %gate.1), channel_id=1, source_target_pairs={{0,17},{1,16},{2,19},{3,18},{4,21},{5,20},{6,23},{7,22},{8,25},{9,... | collective-permute-start | bytes 835592 | tf_op jit(solution)/shard_map/ppermute | solution.py:379
  72.6 3.3 %collective-permute-done.7.refs_1_ = bf16[272,512]{1,0:T(8,128)(2,1)S(1)} collective-permute-done((bf16[272,512]{1,0:T(8,128)(2,1)S(1)}, bf16[272,512]{1,0:T(8,128)(2,1)S(1)}, u32[]{:S(2)}, u32[]{:S(2)}) %collective-permute-start.7) | collective-permute-done | bytes 278560 | tf_op jit(solution)/shard_map/ppermute | solution.py:379
  76.0 9.8 %collective-permute-start.9 = (bf16[272,512]{1,0:T(8,128)(2,1)S(1)}, bf16[272,512]{1,0:T(8,128)(2,1)S(1)}, u32[]{:S(2)}, u32[]{:S(2)}) collective-permute-start(bf16[272,512]{1,0:T(8,128)(2,1)S(1)} %collective-permute-done.7.refs_1_), channel_id=1, source_target_pairs={{0,16},{16,0},{32,48},{48,32},{64,80},{80,64},{96,112},{112,96},{1... | collective-permute-start | bytes 835592 | tf_op jit(solution)/shard_map/ppermute | solution.py:381
  85.8 0.0 collective-permute-done.6.refs_0_.sign_ref
  85.8 1.0 collective-permute-done.8.refs_2_
  86.8 6.0 %collective-permute-done.9.refs_3_ = bf16[272,512]{1,0:T(8,128)(2,1)S(1)} collective-permute-done((bf16[272,512]{1,0:T(8,128)(2,1)S(1)}, bf16[272,512]{1,0:T(8,128)(2,1)S(1)}, u32[]{:S(2)}, u32[]{:S(2)}) %collective-permute-start.9) | collective-permute-done | bytes 278560 | tf_op jit(solution)/shard_map/ppermute | solution.py:381
  92.7 3.9 %all-to-all-done.1.refs_4_ = bf16[8,2,512,128]{3,2,1,0:T(8,128)(2,1)S(1)} async-done(((bf16[8,2,512,128]{3,2,1,0:T(8,128)(2,1)}), bf16[8,2,512,128]{3,2,1,0:T(8,128)(2,1)S(1)}, u32[]{:S(2)}, u32[]{:S(2)}) %all-to-all-start.1) | async-done | bytes 2097184 | tf_op jit(solution)/shard_map/all_to_all | solution.py:375
  96.6 1.3 %product.1 = bf16[4,2,256,256]{3,2,1,0:T(8,128)(2,1)S(1)} custom-call(bf16[272,512]{1,0:T(8,128)(2,1)S(1)} %collective-permute-done.6.refs_0_.sign_ref, bf16[272,512]{1,0:T(8,128)(2,1)S(1)} %collective-permute-done.7.refs_1_, bf16[272,512]{1,0:T(8,128)(2,1)S(1)} %collective-permute-done.8.refs_2_, bf16[272,512]{1,0:T(8,128)(2,1)S(1)} %collective-permute-done.9.refs_3_, ...), custom_call_target="tpu_custom_call" | custom-call | flops 1 | bytes 1 | tf_op jit(solution)/shard_map/product/pallas_call | solution.py:315
  97.9 20.2 %all_to_all.15.in_ref = bf16[8,256,256]{2,1,0:T(8,128)(2,1)S(1)} all-to-all(bf16[8,256,256]{2,1,0:T(8,128)(2,1)S(1)} %bitcast.3), channel_id=1, replica_groups={{0,16,4,20,8,24,12,28},{2,18,6,22,10,26,14,30},{32,48,36,52,40,56,44,60..., dimensions={0} | all-to-all | bytes 2097152 | tf_op jit(solution)/shard_map/all_to_all | solution.py:384
  118.1 1.3 %rotate.1 = bf16[256,512]{1,0:T(8,128)(2,1)} custom-call(bf16[8,256,256]{2,1,0:T(8,128)(2,1)S(1)} %all_to_all.15.in_ref, bf16[272,512]{1,0:T(8,128)(2,1)S(1)} %collective-permute-done.6.refs_0_.sign_ref), custom_call_target="tpu_custom_call" | custom-call | flops 1 | bytes 1 | tf_op jit(solution)/shard_map/rotate/pallas_call | solution.py:326
Async XLA Ops:
  0.0 20.2 %collective-permute-start.1 = (bf16[512,128]{1,0:T(8,128)(2,1)}, bf16[512,128]{1,0:T(8,128)(2,1)S(1)}, u32[]{:S(2)}, u32[]{:S(2)}) collective-permute-start(bf16[512,128]{1,0:T(8,128)(2,1)} %bitcast.4), channel_id=1, source_target_pairs={{0,1},{1,0},{2,65},{3,64},{4,5},{5,4},{6,69},{7,68},{8,9},{9,8},{1... | collective-permute-start | bytes 393224 | tf_op jit(solution)/shard_map/ppermute | solution.py:369
  4.2 16.1 %collective-permute-start.2 = (bf16[512,128]{1,0:T(8,128)(2,1)}, bf16[512,128]{1,0:T(8,128)(2,1)S(1)}, u32[]{:S(2)}, u32[]{:S(2)}) collective-permute-start(bf16[512,128]{1,0:T(8,128)(2,1)} %bitcast.5), channel_id=1, source_target_pairs={{0,33},{1,32},{2,97},{3,96},{4,37},{5,36},{6,101},{7,100},{8,41},{... | collective-permute-start | bytes 393224 | tf_op jit(solution)/shard_map/ppermute | solution.py:369
  12.8 0.7 copy-start
  13.5 6.0 %collective-permute-start = (bf16[3,16,512]{2,1,0:T(8,128)(2,1)S(1)}, bf16[3,16,512]{2,1,0:T(8,128)(2,1)S(1)}, u32[]{:S(2)}, u32[]{:S(2)}) collective-permute-start(bf16[3,16,512]{2,1,0:T(8,128)(2,1)S(1)} %get-tuple-element.23), channel_id=1, source_target_pairs={{0,16},{16,32},{32,48},{48,64},{64,80},{80,96},{96,112},{112,128},... | collective-permute-start | bytes 147464 | tf_op jit(solution)/shard_map/ppermute | solution.py:368
  20.3 22.5 %all-to-all-start = ((f32[8,16,512]{2,1,0:T(8,128)}), f32[8,16,512]{2,1,0:T(8,128)S(1)}, u32[]{:S(2)}, u32[]{:S(2)}) async-start(f32[8,16,512]{2,1,0:T(8,128)} %get-tuple-element.28), calls=%async_computation | async-start | bytes 524288 | tf_op jit(solution)/shard_map/all_to_all | solution.py:372
  42.7 53.9 %all-to-all-start.1 = ((bf16[8,2,512,128]{3,2,1,0:T(8,128)(2,1)}), bf16[8,2,512,128]{3,2,1,0:T(8,128)(2,1)S(1)}, u32[]{:S(2)}, u32[]{:S(2)}) async-start(bf16[8,2,512,128]{3,2,1,0:T(8,128)(2,1)} %fan.1), calls=%async_computation.1 | async-start | bytes 4194304 | tf_op jit(solution)/shard_map/all_to_all | solution.py:375
  46.4 11.0 %collective-permute-start.3 = (f32[16,512]{1,0:T(8,128)S(1)}, f32[16,512]{1,0:T(8,128)S(1)}, u32[]{:S(2)}, u32[]{:S(2)}) collective-permute-start(f32[16,512]{1,0:T(8,128)S(1)} %get-tuple-element.33), channel_id=1, source_target_pairs={{0,16},{16,0},{32,48},{48,32},{64,80},{80,64},{96,112},{112,96},{1... | collective-permute-start | bytes 98312 | tf_op jit(solution)/shard_map/ppermute | solution.py:377
  52.1 6.7 %collective-permute-start.4 = (f32[16,512]{1,0:T(8,128)S(1)}, f32[16,512]{1,0:T(8,128)S(1)}, u32[]{:S(2)}, u32[]{:S(2)}) collective-permute-start(f32[16,512]{1,0:T(8,128)S(1)} %get-tuple-element.34), channel_id=1, source_target_pairs={{0,32},{16,48},{32,0},{48,16},{64,96},{80,112},{96,64},{112,80},{1... | collective-permute-start | bytes 98312 | tf_op jit(solution)/shard_map/ppermute | solution.py:377
  54.0 5.8 %collective-permute-start.5 = (f32[16,512]{1,0:T(8,128)S(1)}, f32[16,512]{1,0:T(8,128)S(1)}, u32[]{:S(2)}, u32[]{:S(2)}) collective-permute-start(f32[16,512]{1,0:T(8,128)S(1)} %get-tuple-element.35), channel_id=1, source_target_pairs={{0,48},{16,32},{32,16},{48,0},{64,112},{80,96},{96,80},{112,64},{1... | collective-permute-start | bytes 98312 | tf_op jit(solution)/shard_map/ppermute | solution.py:377
  59.8 1.0 copy-start.1
  64.1 11.9 %collective-permute-start.7 = (bf16[272,512]{1,0:T(8,128)(2,1)S(1)}, bf16[272,512]{1,0:T(8,128)(2,1)S(1)}, u32[]{:S(2)}, u32[]{:S(2)}) collective-permute-start(bf16[272,512]{1,0:T(8,128)(2,1)S(1)} %gate.1), channel_id=1, source_target_pairs={{0,3},{1,2},{2,1},{3,0},{4,7},{5,6},{6,5},{7,4},{8,11},{9,10},{10,... | collective-permute-start | bytes 835592 | tf_op jit(solution)/shard_map/ppermute | solution.py:379
  66.0 19.8 %collective-permute-start.6 = (bf16[272,512]{1,0:T(8,128)(2,1)S(1)}, bf16[272,512]{1,0:T(8,128)(2,1)S(1)}, u32[]{:S(2)}, u32[]{:S(2)}) collective-permute-start(bf16[272,512]{1,0:T(8,128)(2,1)S(1)} %gate.1), channel_id=1, source_target_pairs={{0,1},{1,0},{2,3},{3,2},{4,5},{5,4},{6,7},{7,6},{8,9},{9,8},{10,11... | collective-permute-start | bytes 835592 | tf_op jit(solution)/shard_map/ppermute | solution.py:379
  68.7 18.0 %collective-permute-start.8 = (bf16[272,512]{1,0:T(8,128)(2,1)S(1)}, bf16[272,512]{1,0:T(8,128)(2,1)S(1)}, u32[]{:S(2)}, u32[]{:S(2)}) collective-permute-start(bf16[272,512]{1,0:T(8,128)(2,1)S(1)} %gate.1), channel_id=1, source_target_pairs={{0,17},{1,16},{2,19},{3,18},{4,21},{5,20},{6,23},{7,22},{8,25},{9,... | collective-permute-start | bytes 835592 | tf_op jit(solution)/shard_map/ppermute | solution.py:379
  76.0 16.8 %collective-permute-start.9 = (bf16[272,512]{1,0:T(8,128)(2,1)S(1)}, bf16[272,512]{1,0:T(8,128)(2,1)S(1)}, u32[]{:S(2)}, u32[]{:S(2)}) collective-permute-start(bf16[272,512]{1,0:T(8,128)(2,1)S(1)} %collective-permute-done.7.refs_1_), channel_id=1, source_target_pairs={{0,16},{16,0},{32,48},{48,32},{64,80},{80,64},{96,112},{112,96},{1... | collective-permute-start | bytes 835592 | tf_op jit(solution)/shard_map/ppermute | solution.py:381

commit v3 on v2

--- a/solution.py
+++ b/solution.py
@@ -71,7 +71,7 @@
             x = mixed_ref[pl.ds(group * rows + i, SUBS, stride=step), :]
             return tuple(a * h + x for a, h in zip(factors, state))
 
-        state = lax.fori_loop(0, step, advance, tuple(jnp.zeros((SUBS, LANES), f32) for _ in range(MODES)), unroll=4)
+        state = lax.fori_loop(0, step, advance, tuple(jnp.zeros((SUBS, LANES), f32) for _ in range(MODES)), unroll=8)
         for m in range(MODES):
             before_ref[group, m] = state[m]
         over = jnp.exp(-decay * step)
@@ -170,7 +170,7 @@
 
         state = advance(0, tuple(state), fix[0], fix[2:4])
         state = advance(1, state, fix[1], fix[4:5])
-        lax.fori_loop(2, step, advance, state, unroll=2)
+        lax.fori_loop(2, step, advance, state, unroll=6)
     for group in range(GROUPS):
         out_ref[0:rows, group * LANES : (group + 1) * LANES] = gated[group * rows : (group + 1) * rows, :].astype(bf16)
     sign = (2 * sign_ref[...] - 1).astype(f32)
@@ -208,13 +208,14 @@
 
 def rotate_kernel(in_ref, sign_ref, out_ref):
     rows = out_ref.shape[0]
-    chunk = 64
+    chunk = 128
     row = lax.broadcasted_iota(jnp.int32, (LANES, LANES), 0)
     column = lax.broadcasted_iota(jnp.int32, (LANES, LANES), 1)
     parity = row & column
     for shift in (4, 2, 1):
         parity = parity ^ (parity >> shift)
     matrix = (1 - 2 * (parity & 1)).astype(f32).astype(bf16)
+    matrix = jnp.concatenate([matrix, matrix], axis=0)
     sign = sign_ref[rows : rows + EDGE, :].astype(f32)[0:1, :]
     for start in range(0, rows, chunk):
         here = slice(start, start + chunk)
@@ -232,12 +233,8 @@
             parts = [parts[i] + parts[i ^ bit] if not i & bit else parts[i ^ bit] - parts[i] for i in range(len(parts))]
         for tile, part in enumerate(parts):
             high = part.astype(bf16)
-            rest = part - high.astype(f32)
-            middle = rest.astype(bf16)
-            low = (rest - middle.astype(f32)).astype(bf16)
-            turned = jnp.dot(low, matrix, preferred_element_type=f32)
-            turned = turned + jnp.dot(middle, matrix, preferred_element_type=f32)
-            turned = turned + jnp.dot(high, matrix, preferred_element_type=f32)
+            middle = (part - high.astype(f32)).astype(bf16)
+            turned = jnp.dot(jnp.concatenate([high, middle], axis=1), matrix, preferred_element_type=f32)
             out_ref[here, tile * LANES : (tile + 1) * LANES] = (turned * (1.0 / math.sqrt(HB))).astype(bf16)
 
 

time: 120 us -> 120 us (level)
  no operation moved by 1% of the time
where the time goes in v3:
time: 120 us; the launch traced here: 119 us
  starting transfers between devices  55.8 us (46%)
  waiting for transfers between devices  29.8 us (25%)
  blocking collectives  20.2 us (17%)
  Pallas kernels  10.9 us (9%)
  local copies, waits for them, and re-layouts  2.39 us (2%)
    all_to_all x1, blocking collectives, shards(): lax.all_to_all(partials.reshape(2 * X, rows, -1), BOTH, 0, 0, axis_index_...  20.2 us
    ppermute x3, starting transfers between devices, shards(): lax.ppermute(carry[turn], 'context', state_route(turn))  10.8 us
    all_to_all x1, waiting for transfers between devices, shards(): lax.all_to_all(packets, 'context', 0, 0, axis_index_groups=Z_GROUPS)  10.5 us
    all_to_all x1, starting transfers between devices, shards(): lax.all_to_all(packets, 'context', 0, 0, axis_index_groups=Z_GROUPS)  10.3 us
    ppermute x1, starting transfers between devices, shards(): blocks.append(lax.ppermute(blocks[1], 'context', pair))  9.77 us
    ppermute x2, starting transfers between devices, shards(): lax.ppermute(out_weight[0], ALL, weight_route(turn))  8.79 us
    ppermute x3, starting transfers between devices, shards(): lax.ppermute(gated, ALL, row_route(*turn))  8.55 us
    ppermute x1, waiting for transfers between devices, shards(): blocks.append(lax.ppermute(blocks[1], 'context', pair))  5.97 us
  transfers between devices with their start and end apart: 12, of which 9 were waited for; matrix products, arithmetic and copies ran while one was open for 1% of the time, Pallas kernels for 7%

profile of v3, /device:TPU:40, one launch (start us, length us, event | category | flops | bytes accessed | tf_op | source)
XLA Modules:
  0.0 119.2 jit_solution(17127777668164324265)
XLA Ops:
  0.0 4.2 %collective-permute-start.1 = (bf16[512,128]{1,0:T(8,128)(2,1)}, bf16[512,128]{1,0:T(8,128)(2,1)S(1)}, u32[]{:S(2)}, u32[]{:S(2)}) collective-permute-start(bf16[512,128]{1,0:T(8,128)(2,1)} %bitcast.4), channel_id=1, source_target_pairs={{0,1},{1,0},{2,65},{3,64},{4,5},{5,4},{6,69},{7,68},{8,9},{9,8},{1... | collective-permute-start | bytes 393224 | tf_op jit(solution)/shard_map/ppermute | solution.py:366
  4.2 4.6 %collective-permute-start.2 = (bf16[512,128]{1,0:T(8,128)(2,1)}, bf16[512,128]{1,0:T(8,128)(2,1)S(1)}, u32[]{:S(2)}, u32[]{:S(2)}) collective-permute-start(bf16[512,128]{1,0:T(8,128)(2,1)} %bitcast.5), channel_id=1, source_target_pairs={{0,33},{1,32},{2,97},{3,96},{4,37},{5,36},{6,101},{7,100},{8,41},{... | collective-permute-start | bytes 393224 | tf_op jit(solution)/shard_map/ppermute | solution.py:366
  8.8 0.7 copy.9.filter_ref
  9.5 3.1 %states.1 = (f32[1024,128]{1,0:T(8,128)S(1)}, f32[1024,128]{1,0:T(8,128)S(1)}, f32[4,16,8,128]{3,2,1,0:T(8,128)S(1)}, f32[16,512]{1,0:T(8,128)S(1)}, f32[3,8,512...) custom-call(bf16[1,256,512]{2,1,0:T(8,128)(2,1)} %q_ref.1, bf16[1,256,512]{2,1,0:T(8,128)(2,1)} %k_ref.1, ...), custom_call_target="tpu_custom_call" | custom-call | flops 1 | bytes 1 | tf_op jit(solution)/shard_map/states/pallas_call | solution.py:248
  12.6 0.0 copy-start
  12.7 0.7 copy-done
  13.4 3.9 %collective-permute-start = (bf16[3,16,512]{2,1,0:T(8,128)(2,1)S(1)}, bf16[3,16,512]{2,1,0:T(8,128)(2,1)S(1)}, u32[]{:S(2)}, u32[]{:S(2)}) collective-permute-start(bf16[3,16,512]{2,1,0:T(8,128)(2,1)S(1)} %get-tuple-element.23), channel_id=1, source_target_pairs={{0,16},{16,32},{32,48},{48,64},{64,80},{80,96},{96,112},{112,128},... | collective-permute-start | bytes 147464 | tf_op jit(solution)/shard_map/ppermute | solution.py:365
  17.3 2.0 %collective-permute-done.halo_ref = bf16[3,16,512]{2,1,0:T(8,128)(2,1)S(1)} collective-permute-done((bf16[3,16,512]{2,1,0:T(8,128)(2,1)S(1)}, bf16[3,16,512]{2,1,0:T(8,128)(2,1)S(1)}, u32[]{:S(2)}, u32[]{:S(2)}) %collective-permute-start) | collective-permute-done | bytes 49184 | tf_op jit(solution)/shard_map/ppermute | solution.py:365
  19.3 0.7 packet.1
  20.1 0.0 collective-permute-done.1.first_ref
  20.1 0.2 collective-permute-done.2.second_ref
  20.3 10.3 %all-to-all-start = ((f32[8,16,512]{2,1,0:T(8,128)}), f32[8,16,512]{2,1,0:T(8,128)S(1)}, u32[]{:S(2)}, u32[]{:S(2)}) async-start(f32[8,16,512]{2,1,0:T(8,128)} %get-tuple-element.28), calls=%async_computation | async-start | bytes 524288 | tf_op jit(solution)/shard_map/all_to_all | solution.py:369
  30.6 1.6 %fan.1 = bf16[8,2,512,128]{3,2,1,0:T(8,128)(2,1)} custom-call(bf16[512,128]{1,0:T(8,128)(2,1)S(1)} %collective-permute-done.1.first_ref, bf16[512,128]{1,0:T(8,128)(2,1)S(1)} %collective-permute-done.2.second_ref), custom_call_target="tpu_custom_call" | custom-call | flops 1 | bytes 1 | tf_op jit(solution)/shard_map/fan/pallas_call | solution.py:278
  32.2 10.5 %all-to-all-done.refs_0_ = f32[8,16,512]{2,1,0:T(8,128)S(1)} async-done(((f32[8,16,512]{2,1,0:T(8,128)}), f32[8,16,512]{2,1,0:T(8,128)S(1)}, u32[]{:S(2)}, u32[]{:S(2)}) %all-to-all-start) | async-done | bytes 262176 | tf_op jit(solution)/shard_map/all_to_all | solution.py:369
  42.7 3.6 %all-to-all-start.1 = ((bf16[8,2,512,128]{3,2,1,0:T(8,128)(2,1)}), bf16[8,2,512,128]{3,2,1,0:T(8,128)(2,1)S(1)}, u32[]{:S(2)}, u32[]{:S(2)}) async-start(bf16[8,2,512,128]{3,2,1,0:T(8,128)(2,1)} %fan.1), calls=%async_computation.1 | async-start | bytes 4194304 | tf_op jit(solution)/shard_map/all_to_all | solution.py:372
  46.3 0.1 carries.1
  46.4 5.5 %collective-permute-start.3 = (f32[16,512]{1,0:T(8,128)S(1)}, f32[16,512]{1,0:T(8,128)S(1)}, u32[]{:S(2)}, u32[]{:S(2)}) collective-permute-start(f32[16,512]{1,0:T(8,128)S(1)} %get-tuple-element.33), channel_id=1, source_target_pairs={{0,16},{16,0},{32,48},{48,32},{64,80},{80,64},{96,112},{112,96},{1... | collective-permute-start | bytes 98312 | tf_op jit(solution)/shard_map/ppermute | solution.py:374
  52.0 1.9 %collective-permute-start.4 = (f32[16,512]{1,0:T(8,128)S(1)}, f32[16,512]{1,0:T(8,128)S(1)}, u32[]{:S(2)}, u32[]{:S(2)}) collective-permute-start(f32[16,512]{1,0:T(8,128)S(1)} %get-tuple-element.34), channel_id=1, source_target_pairs={{0,32},{16,48},{32,0},{48,16},{64,96},{80,112},{96,64},{112,80},{1... | collective-permute-start | bytes 98312 | tf_op jit(solution)/shard_map/ppermute | solution.py:374
  53.9 3.4 %collective-permute-start.5 = (f32[16,512]{1,0:T(8,128)S(1)}, f32[16,512]{1,0:T(8,128)S(1)}, u32[]{:S(2)}, u32[]{:S(2)}) collective-permute-start(f32[16,512]{1,0:T(8,128)S(1)} %get-tuple-element.35), channel_id=1, source_target_pairs={{0,48},{16,32},{32,16},{48,0},{64,112},{80,96},{96,80},{112,64},{1... | collective-permute-start | bytes 98312 | tf_op jit(solution)/shard_map/ppermute | solution.py:374
  57.3 0.0 collective-permute-done.3.carry1
  57.3 1.4 %collective-permute-done.4.carry2 = f32[16,512]{1,0:T(8,128)S(1)} collective-permute-done((f32[16,512]{1,0:T(8,128)S(1)}, f32[16,512]{1,0:T(8,128)S(1)}, u32[]{:S(2)}, u32[]{:S(2)}) %collective-permute-start.4) | collective-permute-done | bytes 32800 | tf_op jit(solution)/shard_map/ppermute | solution.py:374
  58.7 1.0 collective-permute-done.5.carry3
  59.7 0.0 copy-start.1
  59.7 0.9 copy-done.1
  60.7 3.0 %gate.1 = bf16[272,512]{1,0:T(8,128)(2,1)S(1)} custom-call(f32[16,512]{1,0:T(8,128)S(1)} %get-tuple-element.32.carry0, f32[16,512]{1,0:T(8,128)S(1)} %collective-permute-done.3.carry1, f32[16,512]{1,0:T(8,128)S(1)} %collective-permute-done.4.carry2, f32[16,512]{1,0:T(8,128)S(1)} %collective-permute-done.5.carry3, ...), custom_call_target="tpu_custom_call" | custom-call | flops 1 | bytes 1 | tf_op jit(solution)/shard_map/gate/pallas_call | solution.py:300
  63.7 1.9 %collective-permute-start.7 = (bf16[272,512]{1,0:T(8,128)(2,1)S(1)}, bf16[272,512]{1,0:T(8,128)(2,1)S(1)}, u32[]{:S(2)}, u32[]{:S(2)}) collective-permute-start(bf16[272,512]{1,0:T(8,128)(2,1)S(1)} %gate.1), channel_id=1, source_target_pairs={{0,3},{1,2},{2,1},{3,0},{4,7},{5,6},{6,5},{7,4},{8,11},{9,10},{10,... | collective-permute-start | bytes 835592 | tf_op jit(solution)/shard_map/ppermute | solution.py:376
  65.6 2.7 %collective-permute-start.6 = (bf16[272,512]{1,0:T(8,128)(2,1)S(1)}, bf16[272,512]{1,0:T(8,128)(2,1)S(1)}, u32[]{:S(2)}, u32[]{:S(2)}) collective-permute-start(bf16[272,512]{1,0:T(8,128)(2,1)S(1)} %gate.1), channel_id=1, source_target_pairs={{0,1},{1,0},{2,3},{3,2},{4,5},{5,4},{6,7},{7,6},{8,9},{9,8},{10,11... | collective-permute-start | bytes 835592 | tf_op jit(solution)/shard_map/ppermute | solution.py:376
  68.3 3.9 %collective-permute-start.8 = (bf16[272,512]{1,0:T(8,128)(2,1)S(1)}, bf16[272,512]{1,0:T(8,128)(2,1)S(1)}, u32[]{:S(2)}, u32[]{:S(2)}) collective-permute-start(bf16[272,512]{1,0:T(8,128)(2,1)S(1)} %gate.1), channel_id=1, source_target_pairs={{0,17},{1,16},{2,19},{3,18},{4,21},{5,20},{6,23},{7,22},{8,25},{9,... | collective-permute-start | bytes 835592 | tf_op jit(solution)/shard_map/ppermute | solution.py:376
  72.2 3.3 %collective-permute-done.7.refs_1_ = bf16[272,512]{1,0:T(8,128)(2,1)S(1)} collective-permute-done((bf16[272,512]{1,0:T(8,128)(2,1)S(1)}, bf16[272,512]{1,0:T(8,128)(2,1)S(1)}, u32[]{:S(2)}, u32[]{:S(2)}) %collective-permute-start.7) | collective-permute-done | bytes 278560 | tf_op jit(solution)/shard_map/ppermute | solution.py:376
  75.6 9.8 %collective-permute-start.9 = (bf16[272,512]{1,0:T(8,128)(2,1)S(1)}, bf16[272,512]{1,0:T(8,128)(2,1)S(1)}, u32[]{:S(2)}, u32[]{:S(2)}) collective-permute-start(bf16[272,512]{1,0:T(8,128)(2,1)S(1)} %collective-permute-done.7.refs_1_), channel_id=1, source_target_pairs={{0,16},{16,0},{32,48},{48,32},{64,80},{80,64},{96,112},{112,96},{1... | collective-permute-start | bytes 835592 | tf_op jit(solution)/shard_map/ppermute | solution.py:378
  85.3 0.0 collective-permute-done.6.refs_0_.sign_ref
  85.4 1.0 collective-permute-done.8.refs_2_
  86.4 6.0 %collective-permute-done.9.refs_3_ = bf16[272,512]{1,0:T(8,128)(2,1)S(1)} collective-permute-done((bf16[272,512]{1,0:T(8,128)(2,1)S(1)}, bf16[272,512]{1,0:T(8,128)(2,1)S(1)}, u32[]{:S(2)}, u32[]{:S(2)}) %collective-permute-start.9) | collective-permute-done | bytes 278560 | tf_op jit(solution)/shard_map/ppermute | solution.py:378
  92.3 4.3 %all-to-all-done.1.refs_4_ = bf16[8,2,512,128]{3,2,1,0:T(8,128)(2,1)S(1)} async-done(((bf16[8,2,512,128]{3,2,1,0:T(8,128)(2,1)}), bf16[8,2,512,128]{3,2,1,0:T(8,128)(2,1)S(1)}, u32[]{:S(2)}, u32[]{:S(2)}) %all-to-all-start.1) | async-done | bytes 2097184 | tf_op jit(solution)/shard_map/all_to_all | solution.py:372
  96.6 1.3 %product.1 = bf16[4,2,256,256]{3,2,1,0:T(8,128)(2,1)S(1)} custom-call(bf16[272,512]{1,0:T(8,128)(2,1)S(1)} %collective-permute-done.6.refs_0_.sign_ref, bf16[272,512]{1,0:T(8,128)(2,1)S(1)} %collective-permute-done.7.refs_1_, bf16[272,512]{1,0:T(8,128)(2,1)S(1)} %collective-permute-done.8.refs_2_, bf16[272,512]{1,0:T(8,128)(2,1)S(1)} %collective-permute-done.9.refs_3_, ...), custom_call_target="tpu_custom_call" | custom-call | flops 1 | bytes 1 | tf_op jit(solution)/shard_map/product/pallas_call | solution.py:312
  97.9 20.2 %all_to_all.15.in_ref = bf16[8,256,256]{2,1,0:T(8,128)(2,1)S(1)} all-to-all(bf16[8,256,256]{2,1,0:T(8,128)(2,1)S(1)} %bitcast.3), channel_id=1, replica_groups={{0,16,4,20,8,24,12,28},{2,18,6,22,10,26,14,30},{32,48,36,52,40,56,44,60..., dimensions={0} | all-to-all | bytes 2097152 | tf_op jit(solution)/shard_map/all_to_all | solution.py:381
  118.1 1.1 rotate.1
Async XLA Ops:
  0.0 20.1 %collective-permute-start.1 = (bf16[512,128]{1,0:T(8,128)(2,1)}, bf16[512,128]{1,0:T(8,128)(2,1)S(1)}, u32[]{:S(2)}, u32[]{:S(2)}) collective-permute-start(bf16[512,128]{1,0:T(8,128)(2,1)} %bitcast.4), channel_id=1, source_target_pairs={{0,1},{1,0},{2,65},{3,64},{4,5},{5,4},{6,69},{7,68},{8,9},{9,8},{1... | collective-permute-start | bytes 393224 | tf_op jit(solution)/shard_map/ppermute | solution.py:366
  4.2 16.1 %collective-permute-start.2 = (bf16[512,128]{1,0:T(8,128)(2,1)}, bf16[512,128]{1,0:T(8,128)(2,1)S(1)}, u32[]{:S(2)}, u32[]{:S(2)}) collective-permute-start(bf16[512,128]{1,0:T(8,128)(2,1)} %bitcast.5), channel_id=1, source_target_pairs={{0,33},{1,32},{2,97},{3,96},{4,37},{5,36},{6,101},{7,100},{8,41},{... | collective-permute-start | bytes 393224 | tf_op jit(solution)/shard_map/ppermute | solution.py:366
  12.6 0.7 copy-start
  13.4 6.0 %collective-permute-start = (bf16[3,16,512]{2,1,0:T(8,128)(2,1)S(1)}, bf16[3,16,512]{2,1,0:T(8,128)(2,1)S(1)}, u32[]{:S(2)}, u32[]{:S(2)}) collective-permute-start(bf16[3,16,512]{2,1,0:T(8,128)(2,1)S(1)} %get-tuple-element.23), channel_id=1, source_target_pairs={{0,16},{16,32},{32,48},{48,64},{64,80},{80,96},{96,112},{112,128},... | collective-permute-start | bytes 147464 | tf_op jit(solution)/shard_map/ppermute | solution.py:365
  20.3 22.5 %all-to-all-start = ((f32[8,16,512]{2,1,0:T(8,128)}), f32[8,16,512]{2,1,0:T(8,128)S(1)}, u32[]{:S(2)}, u32[]{:S(2)}) async-start(f32[8,16,512]{2,1,0:T(8,128)} %get-tuple-element.28), calls=%async_computation | async-start | bytes 524288 | tf_op jit(solution)/shard_map/all_to_all | solution.py:369
  42.7 53.9 %all-to-all-start.1 = ((bf16[8,2,512,128]{3,2,1,0:T(8,128)(2,1)}), bf16[8,2,512,128]{3,2,1,0:T(8,128)(2,1)S(1)}, u32[]{:S(2)}, u32[]{:S(2)}) async-start(bf16[8,2,512,128]{3,2,1,0:T(8,128)(2,1)} %fan.1), calls=%async_computation.1 | async-start | bytes 4194304 | tf_op jit(solution)/shard_map/all_to_all | solution.py:372
  46.4 10.9 %collective-permute-start.3 = (f32[16,512]{1,0:T(8,128)S(1)}, f32[16,512]{1,0:T(8,128)S(1)}, u32[]{:S(2)}, u32[]{:S(2)}) collective-permute-start(f32[16,512]{1,0:T(8,128)S(1)} %get-tuple-element.33), channel_id=1, source_target_pairs={{0,16},{16,0},{32,48},{48,32},{64,80},{80,64},{96,112},{112,96},{1... | collective-permute-start | bytes 98312 | tf_op jit(solution)/shard_map/ppermute | solution.py:374
  52.0 6.7 %collective-permute-start.4 = (f32[16,512]{1,0:T(8,128)S(1)}, f32[16,512]{1,0:T(8,128)S(1)}, u32[]{:S(2)}, u32[]{:S(2)}) collective-permute-start(f32[16,512]{1,0:T(8,128)S(1)} %get-tuple-element.34), channel_id=1, source_target_pairs={{0,32},{16,48},{32,0},{48,16},{64,96},{80,112},{96,64},{112,80},{1... | collective-permute-start | bytes 98312 | tf_op jit(solution)/shard_map/ppermute | solution.py:374
  53.9 5.8 %collective-permute-start.5 = (f32[16,512]{1,0:T(8,128)S(1)}, f32[16,512]{1,0:T(8,128)S(1)}, u32[]{:S(2)}, u32[]{:S(2)}) collective-permute-start(f32[16,512]{1,0:T(8,128)S(1)} %get-tuple-element.35), channel_id=1, source_target_pairs={{0,48},{16,32},{32,16},{48,0},{64,112},{80,96},{96,80},{112,64},{1... | collective-permute-start | bytes 98312 | tf_op jit(solution)/shard_map/ppermute | solution.py:374
  59.7 1.0 copy-start.1
  63.7 11.9 %collective-permute-start.7 = (bf16[272,512]{1,0:T(8,128)(2,1)S(1)}, bf16[272,512]{1,0:T(8,128)(2,1)S(1)}, u32[]{:S(2)}, u32[]{:S(2)}) collective-permute-start(bf16[272,512]{1,0:T(8,128)(2,1)S(1)} %gate.1), channel_id=1, source_target_pairs={{0,3},{1,2},{2,1},{3,0},{4,7},{5,6},{6,5},{7,4},{8,11},{9,10},{10,... | collective-permute-start | bytes 835592 | tf_op jit(solution)/shard_map/ppermute | solution.py:376
  65.6 19.8 %collective-permute-start.6 = (bf16[272,512]{1,0:T(8,128)(2,1)S(1)}, bf16[272,512]{1,0:T(8,128)(2,1)S(1)}, u32[]{:S(2)}, u32[]{:S(2)}) collective-permute-start(bf16[272,512]{1,0:T(8,128)(2,1)S(1)} %gate.1), channel_id=1, source_target_pairs={{0,1},{1,0},{2,3},{3,2},{4,5},{5,4},{6,7},{7,6},{8,9},{9,8},{10,11... | collective-permute-start | bytes 835592 | tf_op jit(solution)/shard_map/ppermute | solution.py:376
  68.3 18.0 %collective-permute-start.8 = (bf16[272,512]{1,0:T(8,128)(2,1)S(1)}, bf16[272,512]{1,0:T(8,128)(2,1)S(1)}, u32[]{:S(2)}, u32[]{:S(2)}) collective-permute-start(bf16[272,512]{1,0:T(8,128)(2,1)S(1)} %gate.1), channel_id=1, source_target_pairs={{0,17},{1,16},{2,19},{3,18},{4,21},{5,20},{6,23},{7,22},{8,25},{9,... | collective-permute-start | bytes 835592 | tf_op jit(solution)/shard_map/ppermute | solution.py:376
  75.6 16.8 %collective-permute-start.9 = (bf16[272,512]{1,0:T(8,128)(2,1)S(1)}, bf16[272,512]{1,0:T(8,128)(2,1)S(1)}, u32[]{:S(2)}, u32[]{:S(2)}) collective-permute-start(bf16[272,512]{1,0:T(8,128)(2,1)S(1)} %collective-permute-done.7.refs_1_), channel_id=1, source_target_pairs={{0,16},{16,0},{32,48},{48,32},{64,80},{80,64},{96,112},{112,96},{1... | collective-permute-start | bytes 835592 | tf_op jit(solution)/shard_map/ppermute | solution.py:378

commit v4 on v3

--- a/solution.py
+++ b/solution.py
@@ -35,11 +35,13 @@
 
 
 def states_kernel(
-    q_ref, k_ref, v_ref, filter_ref, decay_ref, mixed_ref, query_ref, before_ref, total_ref, first_ref, rate_ref, edge_ref, padded
+    q_ref, k_ref, v_ref, filter_ref, decay_ref, residue_ref, sign_ref, mixed_ref, query_ref, before_ref, total_ref, first_ref, rate_ref, edge_ref, weight_ref, bit_ref, padded
 ):
     rows = mixed_ref.shape[0] // GROUPS
     step = rows // SUBS
     rate_ref[...] = decay_ref[...]
+    weight_ref[...] = residue_ref[...]
+    bit_ref[...] = sign_ref[...]
     padded[0:8, :] = jnp.zeros((8, padded.shape[1]), f32)
     for stream, ref in enumerate((q_ref, k_ref, v_ref)):
         edge_ref[stream] = ref[0, rows - EDGE :, :]
@@ -242,9 +244,9 @@
 PARAMS = pltpu.CompilerParams(vmem_limit_bytes=32 * 1024 * 1024)
 
 
-def states(q, k, v, filters, decay):
+def states(q, k, v, filters, decay, residues, signs):
     rows, width = q.shape[1:]
-    q, k, v, decay = [pltpu.with_memory_space_constraint(a, pltpu.HBM) for a in (q, k, v, decay)]
+    held = [pltpu.with_memory_space_constraint(a, pltpu.HBM) for a in (q, k, v, decay, residues, signs)]
     return pl.pallas_call(
         states_kernel,
         out_shape=(
@@ -255,12 +257,14 @@
             jax.ShapeDtypeStruct((3, 8, width), f32),
             jax.ShapeDtypeStruct(decay.shape, f32),
             jax.ShapeDtypeStruct((3, EDGE, width), bf16),
+            jax.ShapeDtypeStruct(residues.shape, f32),
+            jax.ShapeDtypeStruct(signs.shape, jnp.int32),
         ),
         scratch_shapes=[pltpu.VMEM((rows + 8, width), f32)],
         compiler_params=PARAMS,
         cost_estimate=SMALL,
         name="states",
-    )(q, k, v, filters, decay)
+    )(*held[:3], filters, *held[3:])
 
 
 def packet(halo, firsts, total, filters, decay):
@@ -295,7 +299,6 @@
 
 
 def gate(carry, mixed, query, before, fix, decay, residues, signs):
-    residues, signs = [pltpu.with_memory_space_constraint(a, pltpu.HBM) for a in (residues, signs)]
     before = pltpu.with_memory_space_constraint(before, pltpu.VMEM)
     return pl.pallas_call(
         gate_kernel,
@@ -361,7 +364,9 @@
 
 
 def shards(queries, keys, values, short_filters, decay_rates, residues, out_weight, rotation_signs):
-    mixed, query, before, total, firsts, rates, edge = states(queries, keys, values, short_filters, decay_rates)
+    mixed, query, before, total, firsts, rates, edge, weights, signs = states(
+        queries, keys, values, short_filters, decay_rates, residues, rotation_signs
+    )
     halo = lax.ppermute(edge, "context", [(i, i + 1) for i in range(Z * YL - 1)])
     pieces = [lax.ppermute(out_weight[0], ALL, weight_route(turn)) for turn in range(2)]
     packets, fix = packet(halo, firsts, total, short_filters, rates)
@@ -372,7 +377,7 @@
     weight = lax.all_to_all(weight, "context", 0, 0, axis_index_groups=Z_GROUPS)
     carry = carries(packets, rates)
     carry = [carry[0]] + [lax.ppermute(carry[turn], "context", state_route(turn)) for turn in range(1, YL)]
-    gated = gate(carry, mixed, query, before, fix, rates, residues, rotation_signs)
+    gated = gate(carry, mixed, query, before, fix, rates, weights, signs)
     blocks = [lax.ppermute(gated, ALL, row_route(*turn)) for turn in ((0, 0), (0, 1), (1, 0))]
     pair = [(z * YL + y, z * YL + (y ^ 1)) for z in range(Z) for y in range(YL)]
     blocks.append(lax.ppermute(blocks[1], "context", pair))

time: 120 us -> 120 us (level)
  no operation moved by 1% of the time
where the time goes in v4:
time: 120 us; the launch traced here: 119 us
  starting transfers between devices  55.8 us (46%)
  waiting for transfers between devices  30.4 us (25%)
  blocking collectives  20.2 us (17%)
  Pallas kernels  10.2 us (8%)
  local copies, waits for them, and re-layouts  2.39 us (2%)
    all_to_all x1, blocking collectives, shards(): lax.all_to_all(partials.reshape(2 * X, rows, -1), BOTH, 0, 0, axis_index_...  20.2 us
    ppermute x3, starting transfers between devices, shards(): lax.ppermute(carry[turn], 'context', state_route(turn))  10.9 us
    all_to_all x1, waiting for transfers between devices, shards(): lax.all_to_all(packets, 'context', 0, 0, axis_index_groups=Z_GROUPS)  10.5 us
    all_to_all x1, starting transfers between devices, shards(): lax.all_to_all(packets, 'context', 0, 0, axis_index_groups=Z_GROUPS)  10.3 us
    ppermute x1, starting transfers between devices, shards(): blocks.append(lax.ppermute(blocks[1], 'context', pair))  9.77 us
    ppermute x2, starting transfers between devices, shards(): lax.ppermute(out_weight[0], ALL, weight_route(turn))  8.79 us
    ppermute x3, starting transfers between devices, shards(): lax.ppermute(gated, ALL, row_route(*turn))  8.55 us
    ppermute x1, waiting for transfers between devices, shards(): blocks.append(lax.ppermute(blocks[1], 'context', pair))  5.97 us
  transfers between devices with their start and end apart: 12, of which 9 were waited for; matrix products, arithmetic and copies ran while one was open for 1% of the time, Pallas kernels for 7%

profile of v4, /device:TPU:40, one launch (start us, length us, event | category | flops | bytes accessed | tf_op | source)
XLA Modules:
  0.0 119.2 jit_solution(8834866032374782529)
XLA Ops:
  0.0 4.2 %collective-permute-start.1 = (bf16[512,128]{1,0:T(8,128)(2,1)}, bf16[512,128]{1,0:T(8,128)(2,1)S(1)}, u32[]{:S(2)}, u32[]{:S(2)}) collective-permute-start(bf16[512,128]{1,0:T(8,128)(2,1)} %bitcast.4), channel_id=1, source_target_pairs={{0,1},{1,0},{2,65},{3,64},{4,5},{5,4},{6,69},{7,68},{8,9},{9,8},{1... | collective-permute-start | bytes 393224 | tf_op jit(solution)/shard_map/ppermute | solution.py:371
  4.2 4.6 %collective-permute-start.2 = (bf16[512,128]{1,0:T(8,128)(2,1)}, bf16[512,128]{1,0:T(8,128)(2,1)S(1)}, u32[]{:S(2)}, u32[]{:S(2)}) collective-permute-start(bf16[512,128]{1,0:T(8,128)(2,1)} %bitcast.5), channel_id=1, source_target_pairs={{0,33},{1,32},{2,97},{3,96},{4,37},{5,36},{6,101},{7,100},{8,41},{... | collective-permute-start | bytes 393224 | tf_op jit(solution)/shard_map/ppermute | solution.py:371
  8.8 0.7 copy.9.filter_ref
  9.5 3.2 %states.1 = (f32[1024,128]{1,0:T(8,128)S(1)}, f32[1024,128]{1,0:T(8,128)S(1)}, f32[4,16,8,128]{3,2,1,0:T(8,128)S(1)}, f32[16,512]{1,0:T(8,128)S(1)}, f32[3,8,512...) custom-call(bf16[1,256,512]{2,1,0:T(8,128)(2,1)} %q_ref.1, ...), custom_call_target="tpu_custom_call" | custom-call | flops 1 | bytes 1 | tf_op jit(solution)/shard_map/states/pallas_call | solution.py:250
  12.7 0.0 copy-start
  12.7 0.7 copy-done
  13.4 3.9 %collective-permute-start = (bf16[3,16,512]{2,1,0:T(8,128)(2,1)S(1)}, bf16[3,16,512]{2,1,0:T(8,128)(2,1)S(1)}, u32[]{:S(2)}, u32[]{:S(2)}) collective-permute-start(bf16[3,16,512]{2,1,0:T(8,128)(2,1)S(1)} %get-tuple-element.25), channel_id=1, source_target_pairs={{0,16},{16,32},{32,48},{48,64},{64,80},{80,96},{96,112},{112,128},... | collective-permute-start | bytes 147464 | tf_op jit(solution)/shard_map/ppermute | solution.py:370
  17.4 2.0 %collective-permute-done.halo_ref = bf16[3,16,512]{2,1,0:T(8,128)(2,1)S(1)} collective-permute-done((bf16[3,16,512]{2,1,0:T(8,128)(2,1)S(1)}, bf16[3,16,512]{2,1,0:T(8,128)(2,1)S(1)}, u32[]{:S(2)}, u32[]{:S(2)}) %collective-permute-start) | collective-permute-done | bytes 49184 | tf_op jit(solution)/shard_map/ppermute | solution.py:370
  19.4 0.7 packet.1
  20.1 0.0 collective-permute-done.1.first_ref
  20.1 0.1 collective-permute-done.2.second_ref
  20.3 10.3 %all-to-all-start = ((f32[8,16,512]{2,1,0:T(8,128)}), f32[8,16,512]{2,1,0:T(8,128)S(1)}, u32[]{:S(2)}, u32[]{:S(2)}) async-start(f32[8,16,512]{2,1,0:T(8,128)} %get-tuple-element.30), calls=%async_computation | async-start | bytes 524288 | tf_op jit(solution)/shard_map/all_to_all | solution.py:374
  30.6 1.6 %fan.1 = bf16[8,2,512,128]{3,2,1,0:T(8,128)(2,1)} custom-call(bf16[512,128]{1,0:T(8,128)(2,1)S(1)} %collective-permute-done.1.first_ref, bf16[512,128]{1,0:T(8,128)(2,1)S(1)} %collective-permute-done.2.second_ref), custom_call_target="tpu_custom_call" | custom-call | flops 1 | bytes 1 | tf_op jit(solution)/shard_map/fan/pallas_call | solution.py:282
  32.2 10.5 %all-to-all-done.refs_0_ = f32[8,16,512]{2,1,0:T(8,128)S(1)} async-done(((f32[8,16,512]{2,1,0:T(8,128)}), f32[8,16,512]{2,1,0:T(8,128)S(1)}, u32[]{:S(2)}, u32[]{:S(2)}) %all-to-all-start) | async-done | bytes 262176 | tf_op jit(solution)/shard_map/all_to_all | solution.py:374
  42.7 3.6 %all-to-all-start.1 = ((bf16[8,2,512,128]{3,2,1,0:T(8,128)(2,1)}), bf16[8,2,512,128]{3,2,1,0:T(8,128)(2,1)S(1)}, u32[]{:S(2)}, u32[]{:S(2)}) async-start(bf16[8,2,512,128]{3,2,1,0:T(8,128)(2,1)} %fan.1), calls=%async_computation.1 | async-start | bytes 4194304 | tf_op jit(solution)/shard_map/all_to_all | solution.py:377
  46.3 0.1 carries.1
  46.4 5.6 %collective-permute-start.3 = (f32[16,512]{1,0:T(8,128)S(1)}, f32[16,512]{1,0:T(8,128)S(1)}, u32[]{:S(2)}, u32[]{:S(2)}) collective-permute-start(f32[16,512]{1,0:T(8,128)S(1)} %get-tuple-element.35), channel_id=1, source_target_pairs={{0,16},{16,0},{32,48},{48,32},{64,80},{80,64},{96,112},{112,96},{1... | collective-permute-start | bytes 98312 | tf_op jit(solution)/shard_map/ppermute | solution.py:379
  52.0 1.9 %collective-permute-start.4 = (f32[16,512]{1,0:T(8,128)S(1)}, f32[16,512]{1,0:T(8,128)S(1)}, u32[]{:S(2)}, u32[]{:S(2)}) collective-permute-start(f32[16,512]{1,0:T(8,128)S(1)} %get-tuple-element.36), channel_id=1, source_target_pairs={{0,32},{16,48},{32,0},{48,16},{64,96},{80,112},{96,64},{112,80},{1... | collective-permute-start | bytes 98312 | tf_op jit(solution)/shard_map/ppermute | solution.py:379
  54.0 3.4 %collective-permute-start.5 = (f32[16,512]{1,0:T(8,128)S(1)}, f32[16,512]{1,0:T(8,128)S(1)}, u32[]{:S(2)}, u32[]{:S(2)}) collective-permute-start(f32[16,512]{1,0:T(8,128)S(1)} %get-tuple-element.37), channel_id=1, source_target_pairs={{0,48},{16,32},{32,16},{48,0},{64,112},{80,96},{96,80},{112,64},{1... | collective-permute-start | bytes 98312 | tf_op jit(solution)/shard_map/ppermute | solution.py:379
  57.3 0.0 collective-permute-done.3.carry1
  57.4 1.4 %collective-permute-done.4.carry2 = f32[16,512]{1,0:T(8,128)S(1)} collective-permute-done((f32[16,512]{1,0:T(8,128)S(1)}, f32[16,512]{1,0:T(8,128)S(1)}, u32[]{:S(2)}, u32[]{:S(2)}) %collective-permute-start.4) | collective-permute-done | bytes 32800 | tf_op jit(solution)/shard_map/ppermute | solution.py:379
  58.7 1.0 collective-permute-done.5.carry3
  59.8 0.0 copy-start.1
  59.8 0.9 copy-done.1
  60.7 2.2 %gate.1 = bf16[272,512]{1,0:T(8,128)(2,1)S(1)} custom-call(f32[16,512]{1,0:T(8,128)S(1)} %get-tuple-element.34.carry0, f32[16,512]{1,0:T(8,128)S(1)} %collective-permute-done.3.carry1, f32[16,512]{1,0:T(8,128)S(1)} %collective-permute-done.4.carry2, f32[16,512]{1,0:T(8,128)S(1)} %collective-permute-done.5.carry3, ...), custom_call_target="tpu_custom_call" | custom-call | flops 1 | bytes 1 | tf_op jit(solution)/shard_map/gate/pallas_call | solution.py:303
  63.0 1.9 %collective-permute-start.7 = (bf16[272,512]{1,0:T(8,128)(2,1)S(1)}, bf16[272,512]{1,0:T(8,128)(2,1)S(1)}, u32[]{:S(2)}, u32[]{:S(2)}) collective-permute-start(bf16[272,512]{1,0:T(8,128)(2,1)S(1)} %gate.1), channel_id=1, source_target_pairs={{0,3},{1,2},{2,1},{3,0},{4,7},{5,6},{6,5},{7,4},{8,11},{9,10},{10,... | collective-permute-start | bytes 835592 | tf_op jit(solution)/shard_map/ppermute | solution.py:381
  64.9 2.7 %collective-permute-start.6 = (bf16[272,512]{1,0:T(8,128)(2,1)S(1)}, bf16[272,512]{1,0:T(8,128)(2,1)S(1)}, u32[]{:S(2)}, u32[]{:S(2)}) collective-permute-start(bf16[272,512]{1,0:T(8,128)(2,1)S(1)} %gate.1), channel_id=1, source_target_pairs={{0,1},{1,0},{2,3},{3,2},{4,5},{5,4},{6,7},{7,6},{8,9},{9,8},{10,11... | collective-permute-start | bytes 835592 | tf_op jit(solution)/shard_map/ppermute | solution.py:381
  67.7 3.9 %collective-permute-start.8 = (bf16[272,512]{1,0:T(8,128)(2,1)S(1)}, bf16[272,512]{1,0:T(8,128)(2,1)S(1)}, u32[]{:S(2)}, u32[]{:S(2)}) collective-permute-start(bf16[272,512]{1,0:T(8,128)(2,1)S(1)} %gate.1), channel_id=1, source_target_pairs={{0,17},{1,16},{2,19},{3,18},{4,21},{5,20},{6,23},{7,22},{8,25},{9,... | collective-permute-start | bytes 835592 | tf_op jit(solution)/shard_map/ppermute | solution.py:381
  71.6 3.3 %collective-permute-done.7.refs_1_ = bf16[272,512]{1,0:T(8,128)(2,1)S(1)} collective-permute-done((bf16[272,512]{1,0:T(8,128)(2,1)S(1)}, bf16[272,512]{1,0:T(8,128)(2,1)S(1)}, u32[]{:S(2)}, u32[]{:S(2)}) %collective-permute-start.7) | collective-permute-done | bytes 278560 | tf_op jit(solution)/shard_map/ppermute | solution.py:381
  74.9 9.8 %collective-permute-start.9 = (bf16[272,512]{1,0:T(8,128)(2,1)S(1)}, bf16[272,512]{1,0:T(8,128)(2,1)S(1)}, u32[]{:S(2)}, u32[]{:S(2)}) collective-permute-start(bf16[272,512]{1,0:T(8,128)(2,1)S(1)} %collective-permute-done.7.refs_1_), channel_id=1, source_target_pairs={{0,16},{16,0},{32,48},{48,32},{64,80},{80,64},{96,112},{112,96},{1... | collective-permute-start | bytes 835592 | tf_op jit(solution)/shard_map/ppermute | solution.py:383
  84.7 0.0 collective-permute-done.6.refs_0_.sign_ref
  84.7 1.0 collective-permute-done.8.refs_2_
  85.7 6.0 %collective-permute-done.9.refs_3_ = bf16[272,512]{1,0:T(8,128)(2,1)S(1)} collective-permute-done((bf16[272,512]{1,0:T(8,128)(2,1)S(1)}, bf16[272,512]{1,0:T(8,128)(2,1)S(1)}, u32[]{:S(2)}, u32[]{:S(2)}) %collective-permute-start.9) | collective-permute-done | bytes 278560 | tf_op jit(solution)/shard_map/ppermute | solution.py:383
  91.6 5.0 %all-to-all-done.1.refs_4_ = bf16[8,2,512,128]{3,2,1,0:T(8,128)(2,1)S(1)} async-done(((bf16[8,2,512,128]{3,2,1,0:T(8,128)(2,1)}), bf16[8,2,512,128]{3,2,1,0:T(8,128)(2,1)S(1)}, u32[]{:S(2)}, u32[]{:S(2)}) %all-to-all-start.1) | async-done | bytes 2097184 | tf_op jit(solution)/shard_map/all_to_all | solution.py:377
  96.6 1.3 %product.1 = bf16[4,2,256,256]{3,2,1,0:T(8,128)(2,1)S(1)} custom-call(bf16[272,512]{1,0:T(8,128)(2,1)S(1)} %collective-permute-done.6.refs_0_.sign_ref, bf16[272,512]{1,0:T(8,128)(2,1)S(1)} %collective-permute-done.7.refs_1_, bf16[272,512]{1,0:T(8,128)(2,1)S(1)} %collective-permute-done.8.refs_2_, bf16[272,512]{1,0:T(8,128)(2,1)S(1)} %collective-permute-done.9.refs_3_, ...), custom_call_target="tpu_custom_call" | custom-call | flops 1 | bytes 1 | tf_op jit(solution)/shard_map/product/pallas_call | solution.py:315
  97.9 20.2 %all_to_all.15.in_ref = bf16[8,256,256]{2,1,0:T(8,128)(2,1)S(1)} all-to-all(bf16[8,256,256]{2,1,0:T(8,128)(2,1)S(1)} %bitcast.3), channel_id=1, replica_groups={{0,16,4,20,8,24,12,28},{2,18,6,22,10,26,14,30},{32,48,36,52,40,56,44,60..., dimensions={0} | all-to-all | bytes 2097152 | tf_op jit(solution)/shard_map/all_to_all | solution.py:386
  118.1 1.1 rotate.1
Async XLA Ops:
  0.0 20.1 %collective-permute-start.1 = (bf16[512,128]{1,0:T(8,128)(2,1)}, bf16[512,128]{1,0:T(8,128)(2,1)S(1)}, u32[]{:S(2)}, u32[]{:S(2)}) collective-permute-start(bf16[512,128]{1,0:T(8,128)(2,1)} %bitcast.4), channel_id=1, source_target_pairs={{0,1},{1,0},{2,65},{3,64},{4,5},{5,4},{6,69},{7,68},{8,9},{9,8},{1... | collective-permute-start | bytes 393224 | tf_op jit(solution)/shard_map/ppermute | solution.py:371
  4.2 16.1 %collective-permute-start.2 = (bf16[512,128]{1,0:T(8,128)(2,1)}, bf16[512,128]{1,0:T(8,128)(2,1)S(1)}, u32[]{:S(2)}, u32[]{:S(2)}) collective-permute-start(bf16[512,128]{1,0:T(8,128)(2,1)} %bitcast.5), channel_id=1, source_target_pairs={{0,33},{1,32},{2,97},{3,96},{4,37},{5,36},{6,101},{7,100},{8,41},{... | collective-permute-start | bytes 393224 | tf_op jit(solution)/shard_map/ppermute | solution.py:371
  12.7 0.7 copy-start
  13.4 6.0 %collective-permute-start = (bf16[3,16,512]{2,1,0:T(8,128)(2,1)S(1)}, bf16[3,16,512]{2,1,0:T(8,128)(2,1)S(1)}, u32[]{:S(2)}, u32[]{:S(2)}) collective-permute-start(bf16[3,16,512]{2,1,0:T(8,128)(2,1)S(1)} %get-tuple-element.25), channel_id=1, source_target_pairs={{0,16},{16,32},{32,48},{48,64},{64,80},{80,96},{96,112},{112,128},... | collective-permute-start | bytes 147464 | tf_op jit(solution)/shard_map/ppermute | solution.py:370
  20.3 22.5 %all-to-all-start = ((f32[8,16,512]{2,1,0:T(8,128)}), f32[8,16,512]{2,1,0:T(8,128)S(1)}, u32[]{:S(2)}, u32[]{:S(2)}) async-start(f32[8,16,512]{2,1,0:T(8,128)} %get-tuple-element.30), calls=%async_computation | async-start | bytes 524288 | tf_op jit(solution)/shard_map/all_to_all | solution.py:374
  42.7 53.9 %all-to-all-start.1 = ((bf16[8,2,512,128]{3,2,1,0:T(8,128)(2,1)}), bf16[8,2,512,128]{3,2,1,0:T(8,128)(2,1)S(1)}, u32[]{:S(2)}, u32[]{:S(2)}) async-start(bf16[8,2,512,128]{3,2,1,0:T(8,128)(2,1)} %fan.1), calls=%async_computation.1 | async-start | bytes 4194304 | tf_op jit(solution)/shard_map/all_to_all | solution.py:377
  46.4 10.9 %collective-permute-start.3 = (f32[16,512]{1,0:T(8,128)S(1)}, f32[16,512]{1,0:T(8,128)S(1)}, u32[]{:S(2)}, u32[]{:S(2)}) collective-permute-start(f32[16,512]{1,0:T(8,128)S(1)} %get-tuple-element.35), channel_id=1, source_target_pairs={{0,16},{16,0},{32,48},{48,32},{64,80},{80,64},{96,112},{112,96},{1... | collective-permute-start | bytes 98312 | tf_op jit(solution)/shard_map/ppermute | solution.py:379
  52.0 6.7 %collective-permute-start.4 = (f32[16,512]{1,0:T(8,128)S(1)}, f32[16,512]{1,0:T(8,128)S(1)}, u32[]{:S(2)}, u32[]{:S(2)}) collective-permute-start(f32[16,512]{1,0:T(8,128)S(1)} %get-tuple-element.36), channel_id=1, source_target_pairs={{0,32},{16,48},{32,0},{48,16},{64,96},{80,112},{96,64},{112,80},{1... | collective-permute-start | bytes 98312 | tf_op jit(solution)/shard_map/ppermute | solution.py:379
  54.0 5.8 %collective-permute-start.5 = (f32[16,512]{1,0:T(8,128)S(1)}, f32[16,512]{1,0:T(8,128)S(1)}, u32[]{:S(2)}, u32[]{:S(2)}) collective-permute-start(f32[16,512]{1,0:T(8,128)S(1)} %get-tuple-element.37), channel_id=1, source_target_pairs={{0,48},{16,32},{32,16},{48,0},{64,112},{80,96},{96,80},{112,64},{1... | collective-permute-start | bytes 98312 | tf_op jit(solution)/shard_map/ppermute | solution.py:379
  59.8 1.0 copy-start.1
  63.0 11.9 %collective-permute-start.7 = (bf16[272,512]{1,0:T(8,128)(2,1)S(1)}, bf16[272,512]{1,0:T(8,128)(2,1)S(1)}, u32[]{:S(2)}, u32[]{:S(2)}) collective-permute-start(bf16[272,512]{1,0:T(8,128)(2,1)S(1)} %gate.1), channel_id=1, source_target_pairs={{0,3},{1,2},{2,1},{3,0},{4,7},{5,6},{6,5},{7,4},{8,11},{9,10},{10,... | collective-permute-start | bytes 835592 | tf_op jit(solution)/shard_map/ppermute | solution.py:381
  64.9 19.8 %collective-permute-start.6 = (bf16[272,512]{1,0:T(8,128)(2,1)S(1)}, bf16[272,512]{1,0:T(8,128)(2,1)S(1)}, u32[]{:S(2)}, u32[]{:S(2)}) collective-permute-start(bf16[272,512]{1,0:T(8,128)(2,1)S(1)} %gate.1), channel_id=1, source_target_pairs={{0,1},{1,0},{2,3},{3,2},{4,5},{5,4},{6,7},{7,6},{8,9},{9,8},{10,11... | collective-permute-start | bytes 835592 | tf_op jit(solution)/shard_map/ppermute | solution.py:381
  67.7 18.0 %collective-permute-start.8 = (bf16[272,512]{1,0:T(8,128)(2,1)S(1)}, bf16[272,512]{1,0:T(8,128)(2,1)S(1)}, u32[]{:S(2)}, u32[]{:S(2)}) collective-permute-start(bf16[272,512]{1,0:T(8,128)(2,1)S(1)} %gate.1), channel_id=1, source_target_pairs={{0,17},{1,16},{2,19},{3,18},{4,21},{5,20},{6,23},{7,22},{8,25},{9,... | collective-permute-start | bytes 835592 | tf_op jit(solution)/shard_map/ppermute | solution.py:381
  74.9 16.8 %collective-permute-start.9 = (bf16[272,512]{1,0:T(8,128)(2,1)S(1)}, bf16[272,512]{1,0:T(8,128)(2,1)S(1)}, u32[]{:S(2)}, u32[]{:S(2)}) collective-permute-start(bf16[272,512]{1,0:T(8,128)(2,1)S(1)} %collective-permute-done.7.refs_1_), channel_id=1, source_target_pairs={{0,16},{16,0},{32,48},{48,32},{64,80},{80,64},{96,112},{112,96},{1... | collective-permute-start | bytes 835592 | tf_op jit(solution)/shard_map/ppermute | solution.py:383
